TPU v7x, 32 devices: a whole 2x2x4 slice. The times are simulated.
32 devices in a mesh: dp: 8 (over z, core), tensor: 4 (over y, x).
Axes of the slice: x: 2, y: 2, z: 4, core: 2. Of those that a mesh axis runs over, the one named last changes fastest.
Arguments:
- grad_query: bfloat16 [2048, 8192], P('dp', 'tensor'), may hold values from -6 to 6
- query_weight: bfloat16 [8192, 8192], P('dp', 'tensor')
- grad_resid: bfloat16 [2048, 8192], P('dp', 'tensor'), may hold values from -6 to 6
- embeds: bfloat16 [2048, 8192], P('dp', 'tensor')
- norm_gain: float32 [8192], P('tensor'), may hold values from 0.1 to 1.9
- img_pos: int32 [8, 128], P('dp'), may hold values from 0 to 255, as said below
- img_count: int32 [8], P('dp'), may hold values from 64 to 128, as said below
- img_dest: int32 [8, 128], P('dp'), may hold values from 0 to 7, as said below
- merge_weight: bfloat16 [5120, 8192], P('dp', 'tensor'), may hold values from -0.0625 to 0.0625
- merge_pre: bfloat16 [1536, 5120], P('dp', 'tensor'), may hold values from -5 to 5
Outputs:
- grad_pre: float32 [1536, 5120], P('dp', 'tensor')
Inputs may be any that keep to these rules, and one draw needn't show every extreme that they name: `img_pos`: positions of one device are distinct. `img_count`: at least 64 on every device; some device has 128. `img_dest`: among the rows of one device no encoder device is named more than 24 times; the first 24 rows of every device name one common encoder device, which so receives 24 live rows from every device.
All inputs are finite; a program needn't handle non-finite values.
Results may differ from a plain program's by a relative error of at most 0.034.
Values may be sent and summed in bfloat16 or wider, within the bound.
A program may use at most 128 MiB of HBM per device.

v0:
```python
import jax
import jax.numpy as jnp
from jax import lax
from jax.sharding import PartitionSpec as P

D = 8192


NORM_EPS = 1e-06


def gelu_slope(pre):
    value = pre.astype(jnp.float32)
    cdf_part = 0.5 * (1.0 + lax.erf(value * 0.7071067811865476))
    pdf_part = jnp.exp(-0.5 * value * value) * 0.3989422804014327
    return cdf_part + value * pdf_part


def transposed_product(left, right):
    return lax.dot_general(
        left, right, (((1,), (1,)), ((), ())), preferred_element_type=jnp.float32
    )


def local(
    grad_query,
    query_weight,
    grad_resid,
    embeds,
    norm_gain,
    img_pos,
    img_count,
    img_dest,
    merge_weight,
    merge_pre,
):
    groups = lax.axis_size("dp")
    capacity = merge_pre.shape[0] // groups
    positions = img_pos[0]
    image_count = positions.shape[0]
    picked = jnp.take(grad_query, positions, axis=0)
    partial_value = transposed_product(
        picked, lax.all_gather(query_weight, "dp", axis=0, tiled=True)
    )
    normal_grad = lax.psum_scatter(
        partial_value.astype(jnp.bfloat16), "tensor", scatter_dimension=1, tiled=True
    ).astype(jnp.float32)
    inputs = jnp.take(embeds, positions, axis=0).astype(jnp.float32)
    residual = jnp.take(grad_resid, positions, axis=0).astype(jnp.float32)
    scaled = norm_gain[None, :] * normal_grad
    squares, inner_sum = lax.psum(
        (jnp.sum(inputs * inputs, axis=1), jnp.sum(scaled * inputs, axis=1)), "tensor"
    )
    inverse = lax.rsqrt(squares / D + NORM_EPS)
    handoff = residual + inverse[:, None] * scaled - inputs * (inverse**3 * inner_sum / D)[:, None]
    handoff = handoff.astype(jnp.bfloat16)
    is_live = jnp.arange(image_count, dtype=jnp.int32) < img_count[0]
    target_dev = img_dest[0]
    dest_hot = (
        (target_dev[:, None] == jnp.arange(groups, dtype=jnp.int32)[None, :]) & is_live[:, None]
    ).astype(jnp.int32)
    earlier = jnp.cumsum(dest_hot, axis=0) - dest_hot
    slot_index = jnp.sum(earlier * dest_hot, axis=1)
    target = jnp.where(is_live, target_dev * capacity + slot_index, -1)
    placing = jnp.arange(groups * capacity, dtype=jnp.int32)[:, None] == target[None, :]
    merge_full = lax.all_gather(merge_weight, "dp", axis=0, tiled=True)
    outbox = jnp.dot(
        placing.astype(jnp.bfloat16), handoff, preferred_element_type=jnp.float32
    ).astype(jnp.bfloat16)
    outbox = outbox.reshape(groups, capacity, handoff.shape[1])
    partial_hidden = jnp.einsum(
        "sjd,hd->sjh",
        lax.all_to_all(outbox, "dp", split_axis=0, concat_axis=0, tiled=True),
        merge_full,
        preferred_element_type=jnp.float32,
    )
    hidden_grad = lax.psum_scatter(
        partial_hidden.astype(jnp.bfloat16), "tensor", scatter_dimension=2, tiled=True
    ).astype(jnp.float32)
    hidden_grad = hidden_grad.reshape(groups * capacity, hidden_grad.shape[2])
    return hidden_grad * gelu_slope(merge_pre)


def solution(mesh):
    in_specs = (
        P("dp", "tensor"),
        P("dp", "tensor"),
        P("dp", "tensor"),
        P("dp", "tensor"),
        P("tensor"),
        P("dp", None),
        P("dp"),
        P("dp", None),
        P("dp", "tensor"),
        P("dp", "tensor"),
    )
    out_specs = P("dp", "tensor")
    return jax.shard_map(local, mesh=mesh, in_specs=in_specs, out_specs=out_specs, check_vma=False)
```

profile of v0, /device:TPU:0, one launch (start us, length us, event | category | flops | bytes accessed | tf_op | source)
XLA Modules:
  0.0 609.1 jit_solution(2632832763575061612)
XLA Ops:
  6.5 0.0 copy-start
  6.5 0.0 copy-start.7
  6.5 0.0 all-gather.3.cloned.1.call-start
  6.5 0.7 all-gather.3.cloned.1.call-update
  7.3 0.0 reduce-scatter.3.cloned.1.call-start
  7.3 0.0 copy-done.7
  7.3 0.4 copy-done
  7.8 0.9 gather_fusion.2
  8.7 291.6 %all-gather.3.cloned.1.call-done = bf16[8192,2048]{1,0:T(8,128)(2,1)} async-done(((bf16[1024,2048]{1,0:T(8,128)(2,1)}), bf16[8192,2048]{1,0:T(8,128)(2,1)}) %all-gather.3.cloned.1.call-update) | async-done | bytes 33554448 | tf_op jit(solution)/shard_map/all_gather | solution.py:43
  300.3 17.0 %convolution_convert_fusion = bf16[128,8192]{1,0:T(8,128)(2,1)} fusion(bf16[8192,2048]{1,0:T(8,128)(2,1)} %all-gather.3.cloned.1.call-done, bf16[128,2048]{1,0:T(8,128)(2,1)S(1)} %gather_fusion.2, pred[128]{0:T(512)(128)(4,1)S(1)} %compare_and_fusion), kind=kOutput, calls=%fused_computation.5 | convolution fusion | flops 4296278016 | bytes 36176000 | tf_op jit(solution)/shard_map/dot_general | solution.py:20
  317.3 0.0 copy-start.2
  317.3 0.0 reduce-scatter.3.cloned.1.call-update
  317.3 0.0 copy-start.3
  317.4 0.0 all-gather.5.cloned.1.call-start
  317.4 0.7 all-gather.5.cloned.1.call-update
  318.1 0.4 copy-done.2
  318.5 0.0 copy-start.6
  318.5 0.0 copy-start.5
  318.5 0.9 gather_fusion.1
  320.1 0.0 copy-done.3
  320.1 0.9 gather_fusion
  321.1 0.0 copy-done.6
  321.1 0.1 fusion.27
  321.2 0.2 reduce_window_sum.11
  321.4 0.2 select_reduce_fusion
  321.6 29.3 %reduce-scatter.3.cloned.1.call-done = bf16[128,2048]{1,0:T(8,128)(2,1)} async-done(((bf16[128,8192]{1,0:T(8,128)(2,1)}), bf16[128,2048]{1,0:T(8,128)(2,1)}) %reduce-scatter.3.cloned.1.call-update) | async-done | bytes 524304 | tf_op jit(solution)/shard_map/reduce_scatter | solution.py:45
  350.9 0.0 copy-done.5
  350.9 1.4 fusion.5
  352.3 8.9 %all-reduce = (f32[128]{0:T(128)S(1)}, f32[128]{0:T(128)S(1)}) all-reduce(f32[128]{0:T(128)S(1)} %get-tuple-element.7, f32[128]{0:T(128)S(1)} %get-tuple-element.6), channel_id=1, replica_groups=mesh['dp'=8,'tensor'=4] {'tensor'}, use_global_device_ids=true, to_apply=%region_6.8 | all-reduce | flops 256 | bytes 2048 | tf_op jit(solution)/shard_map/psum | solution.py:51
  361.3 2.7 convolution_convert_fusion.1
  363.9 4.6 all-to-all-start
  368.5 0.0 copy-start.4
  368.6 0.0 reduce-scatter.5.cloned.1.call-start
  368.6 186.3 %all-gather.5.cloned.1.call-done = bf16[5120,2048]{1,0:T(8,128)(2,1)} async-done(((bf16[640,2048]{1,0:T(8,128)(2,1)}), bf16[5120,2048]{1,0:T(8,128)(2,1)}) %all-gather.5.cloned.1.call-update) | async-done | bytes 20971536 | tf_op jit(solution)/shard_map/all_gather | solution.py:66
  554.9 0.0 all-to-all-done
  554.9 0.0 copy-start.1
  554.9 12.8 %fusion.2 = bf16[8,24,5120]{2,1,0:T(8,128)(2,1)} fusion(bf16[8,24,2048]{2,1,0:T(8,128)(2,1)S(1)} %all-to-all-done, bf16[5120,2048]{1,0:T(8,128)(2,1)} %all-gather.5.cloned.1.call-done), kind=kOutput, calls=%fused_computation.6 | convolution fusion | flops 4027514880 | bytes 23724032 | tf_op jit(solution)/shard_map/sjd,hd->sjh/dot_general | solution.py:71
  567.7 0.0 reduce-scatter.5.cloned.1.call-update
  567.7 32.4 %reduce-scatter.5.cloned.1.call-done = bf16[8,24,1280]{2,1,0:T(8,128)(2,1)} async-done(((bf16[8,24,5120]{2,1,0:T(8,128)(2,1)}), bf16[8,24,1280]{2,1,0:T(8,128)(2,1)}) %reduce-scatter.5.cloned.1.call-update) | async-done | bytes 491536 | tf_op jit(solution)/shard_map/reduce_scatter | solution.py:77
  600.1 0.0 copy-done.4
  600.1 2.4 fusion.13
  602.6 0.0 copy-done.1
  (6 shorter events, 0.0 us)
Async XLA Ops:
  6.5 1.2 copy-start
  6.5 0.8 copy-start.7
  6.5 293.8 %all-gather.3.cloned.1.call-start = ((), (), s32[]{:S(2)}) async-start(), calls=%async_computation.3 | async-start | bytes 37748736 | tf_op jit(solution)/shard_map/all_gather | solution.py:43
  7.3 343.6 %reduce-scatter.3.cloned.1.call-start = ((), (), s32[]{:S(2)}) async-start(), calls=%async_computation.4 | async-start | bytes 2621440 | tf_op jit(solution)/shard_map/reduce_scatter | solution.py:45
  317.3 1.2 copy-start.2
  317.3 2.8 copy-start.3
  317.4 237.6 %all-gather.5.cloned.1.call-start = ((), (), s32[]{:S(2)}) async-start(), calls=%async_computation.5 | async-start | bytes 23592960 | tf_op jit(solution)/shard_map/all_gather | solution.py:66
  318.5 2.6 copy-start.6
  318.5 32.3 %copy-start.5 = (f32[2048]{0:T(1024)S(1)}, f32[2048]{0:T(1024)}, u32[]{:S(2)}) copy-start(f32[2048]{0:T(1024)} %param.16) | copy-start | bytes 24580
  363.9 191.0 %all-to-all-start = ((bf16[8,24,2048]{2,1,0:T(8,128)(2,1)}), bf16[8,24,2048]{2,1,0:T(8,128)(2,1)S(1)}, u32[]{:S(2)}, u32[]{:S(2)}) async-start(bf16[8,24,2048]{2,1,0:T(8,128)(2,1)} %bitcast.5), calls=%async_computation.1 | async-start | bytes 1572864 | tf_op jit(solution)/shard_map/all_to_all | solution.py:73
  368.5 231.6 %copy-start.4 = (bf16[192,1280]{1,0:T(8,128)(2,1)S(1)}, bf16[192,1280]{1,0:T(8,128)(2,1)}, u32[]{:S(2)}) copy-start(bf16[192,1280]{1,0:T(8,128)(2,1)} %param.21) | copy-start | bytes 1474564
  368.6 231.6 %reduce-scatter.5.cloned.1.call-start = ((), (), s32[]{:S(2)}) async-start(), calls=%async_computation.6 | async-start | bytes 2457600 | tf_op jit(solution)/shard_map/reduce_scatter | solution.py:77
  554.9 47.6 %copy-start.1 = (bf16[256,2048]{1,0:T(8,128)(2,1)S(1)}, bf16[256,2048]{1,0:T(8,128)(2,1)}, u32[]{:S(2)}) copy-start(bf16[256,2048]{1,0:T(8,128)(2,1)} %param.12) | copy-start | bytes 3145732
Sparse Core Ops, SparseCore 0:
  9.0 291.3 all-gather.2
  317.5 33.3 reduce-scatter.2
  352.6 202.2 all-gather.4
  567.8 32.2 reduce-scatter.4
where the time goes:
time: 610 us; the launch traced here: 609 us
  waiting for transfers between devices  541 us (89%)
  matrix products  32.4 us (5%)
  between operations  13.9 us (2%)
  blocking collectives  8.93 us (1%)
    all_gather x1, waiting for transfers between devices, local(): lax.all_gather(query_weight, 'dp', axis=0, tiled=True)  292 us
    all_gather x1, waiting for transfers between devices, local(): merge_full = lax.all_gather(merge_weight, 'dp', axis=0, tiled=True)  186 us
    reduce_scatter x1, waiting for transfers between devices, local(): lax.psum_scatter(partial_hidden.astype(jnp.bfloat16), 'tensor', scatter_d...  32.4 us
    reduce_scatter x1, waiting for transfers between devices, local(): lax.psum_scatter(partial_value.astype(jnp.bfloat16), 'tensor', scatter_di...  29.3 us
    dot_general x1, matrix products, transposed_product(): lax.dot_general(left, right, (((1,), (1,)), ((), ())), preferred_element_...  17 us
    dot_general x1, matrix products, local(): jnp.einsum('sjd,hd->sjh', lax.all_to_all(outbox, 'dp', split_axis=0, conc...  12.8 us
  transfers between devices with their start and end apart: 5, of which 4 were waited for; matrix products, arithmetic and copies ran while one was open for 1% of the time, Pallas kernels for 0%

commit v1 on v0

v1 whole, which is shorter than its diff:
```python
import jax
import jax.numpy as jnp
from jax import lax
from jax.sharding import PartitionSpec as P

NORM_EPS = 1e-06


def gelu_slope(pre):
    value = pre.astype(jnp.float32)
    cdf_part = 0.5 * (1.0 + lax.erf(value * 0.7071067811865476))
    pdf_part = jnp.exp(-0.5 * value * value) * 0.3989422804014327
    return cdf_part + value * pdf_part


def transposed_product(left, right):
    return lax.dot_general(
        left, right, (((1,), (1,)), ((), ())), preferred_element_type=jnp.float32
    )


def targets(img_count, img_dest, groups, capacity):
    image_count = img_dest.shape[1]
    is_live = jnp.arange(image_count, dtype=jnp.int32) < img_count[0]
    target_dev = img_dest[0]
    dest_hot = (
        (target_dev[:, None] == jnp.arange(groups, dtype=jnp.int32)[None, :]) & is_live[:, None]
    ).astype(jnp.int32)
    earlier = jnp.cumsum(dest_hot, axis=0) - dest_hot
    slot_index = jnp.sum(earlier * dest_hot, axis=1)
    return jnp.where(is_live, target_dev * capacity + slot_index, -1)


def local(
    grad_query,
    query_weight,
    grad_resid,
    embeds,
    norm_gain,
    img_pos,
    img_count,
    img_dest,
    merge_weight,
    merge_pre,
):
    groups = lax.axis_size("dp")
    parts = lax.axis_size("tensor")
    capacity = merge_pre.shape[0] // groups
    positions = img_pos[0]
    image_count = positions.shape[0]
    rows = image_count // parts
    block = query_weight.shape[0]
    width = block * groups
    picked = lax.all_gather(jnp.take(grad_query, positions, axis=0), "dp", axis=0, tiled=True)
    inputs = jnp.take(embeds, positions, axis=0)
    residual = jnp.take(grad_resid, positions, axis=0)
    inputs = lax.all_to_all(inputs, "tensor", split_axis=0, concat_axis=1, tiled=True)
    residual = lax.all_to_all(residual, "tensor", split_axis=0, concat_axis=1, tiled=True)
    inputs = inputs.astype(jnp.float32)
    gain = lax.all_gather(norm_gain, "tensor", axis=0, tiled=True)
    target = targets(img_count, img_dest, groups, capacity)
    target = lax.all_gather(target, "dp", axis=0)

    partial_value = transposed_product(picked, query_weight).astype(jnp.bfloat16)
    partial_value = partial_value.reshape(groups, parts, rows, block)
    summed = lax.psum_scatter(partial_value, "tensor", scatter_dimension=1, tiled=False)
    normal_grad = lax.all_to_all(summed, "dp", split_axis=0, concat_axis=0, tiled=True)
    normal_grad = normal_grad.transpose(1, 0, 2).reshape(rows, width).astype(jnp.float32)

    scaled = gain[None, :] * normal_grad
    squares = jnp.sum(inputs * inputs, axis=1)
    inner_sum = jnp.sum(scaled * inputs, axis=1)
    inverse = lax.rsqrt(squares / width + NORM_EPS)
    handoff = (
        residual.astype(jnp.float32)
        + inverse[:, None] * scaled
        - inputs * (inverse**3 * inner_sum / width)[:, None]
    )
    handoff = handoff.astype(jnp.bfloat16)
    handoff = lax.all_to_all(handoff, "tensor", split_axis=1, concat_axis=0, tiled=True)
    handoff = lax.all_gather(handoff, "dp", axis=0, tiled=True)

    hidden = transposed_product(handoff, merge_weight).astype(jnp.bfloat16)
    hidden_block = hidden.shape[1]
    hidden = hidden.reshape(groups, image_count, hidden_block)
    placing = jnp.arange(groups * capacity, dtype=jnp.int32)[None, :, None] == target[:, None, :]
    placed = jnp.einsum(
        "spj,sjh->sph", placing.astype(jnp.bfloat16), hidden, preferred_element_type=jnp.float32
    ).astype(jnp.bfloat16)
    placed = placed.reshape(groups, groups, capacity, hidden_block).transpose(1, 0, 2, 3)
    placed = placed.reshape(groups, parts, groups * capacity // parts, hidden_block)
    summed = lax.psum_scatter(placed, "tensor", scatter_dimension=1, tiled=False)
    summed = lax.all_to_all(summed, "dp", split_axis=0, concat_axis=0, tiled=True)
    summed = summed.transpose(1, 0, 2).reshape(groups * capacity // parts, groups * hidden_block)
    hidden_grad = lax.all_to_all(summed, "tensor", split_axis=1, concat_axis=0, tiled=True)
    return hidden_grad.astype(jnp.float32) * gelu_slope(merge_pre)


def solution(mesh):
    in_specs = (
        P("dp", "tensor"),
        P("dp", "tensor"),
        P("dp", "tensor"),
        P("dp", "tensor"),
        P("tensor"),
        P("dp", None),
        P("dp"),
        P("dp", None),
        P("dp", "tensor"),
        P("dp", "tensor"),
    )
    out_specs = P("dp", "tensor")
    return jax.shard_map(local, mesh=mesh, in_specs=in_specs, out_specs=out_specs, check_vma=False)
```

time: 610 us -> 329 us (0.54)
  waiting for transfers between devices: 541 us -> 186 us
  blocking collectives: 8.93 us -> 59.2 us
  local copies, waits for them, and re-layouts: 3.71 us -> 27.9 us
  matrix products: 32.4 us -> 14.3 us
  other arithmetic: 4.36 us -> 13.6 us
  starting transfers between devices: 4.74 us -> 12.7 us
    all_gather x2, waiting for transfers between devices: 478 us -> 83.8 us  [the longest x1 50 us: local(): lax.all_gather(jnp.take(grad_query, positions, axis=0), 'dp', axis=0, til...]
    unnamed x4 -> x6, waiting for transfers between devices: 1.42 us -> 98.7 us
    reduce_scatter x2 -> x0, waiting for transfers between devices: 61.7 us -> none  [the longest x1 32.4 us: local(): lax.psum_scatter(partial_hidden.astype(jnp.bfloat16), 'tensor', scatter_d...]
    all_to_all x0 -> x3, blocking collectives: none -> 40.7 us  [the longest x1 19.1 us: local(): lax.all_to_all(summed, 'dp', split_axis=0, concat_axis=0, tiled=True)]
    all_gather x0 -> x2, blocking collectives: none -> 18.5 us  [the longest x1 10.4 us: local(): target = lax.all_gather(target, 'dp', axis=0)]
    dot_general x2 -> x1, matrix products: 15.4 us -> 0.66 us  [local(): jnp.einsum('spj,sjh->sph', placing.astype(jnp.bfloat16), hidden, preferre...]
    psum x1 -> x0, blocking collectives: 8.93 us -> none  [local(): lax.psum((jnp.sum(inputs * inputs, axis=1), jnp.sum(scaled * inputs, axis...]
    all_to_all x1 -> x3, starting transfers between devices: 4.61 us -> 12.4 us  [the longest x1 4.61 us: local(): lax.all_to_all(summed, 'dp', split_axis=0, concat_axis=0, tiled=True)]
  transfers between devices with their start and end apart: 5 -> 7, of which waited for: 4 -> 6; matrix products, arithmetic and copies ran while one was open for 1% -> 5% of each run, Pallas kernels for 0% -> 0%
where the time goes in v1:
time: 329 us; the launch traced here: 328 us
  waiting for transfers between devices  186 us (57%)
  blocking collectives  59.2 us (18%)
  local copies, waits for them, and re-layouts  27.9 us (8%)
  matrix products  14.3 us (4%)
  between operations  13.9 us (4%)
  other arithmetic  13.6 us (4%)
  starting transfers between devices  12.7 us (4%)
    unnamed x6, waiting for transfers between devices  98.7 us
    all_gather x1, waiting for transfers between devices, local(): lax.all_gather(jnp.take(grad_query, positions, axis=0), 'dp', axis=0, til...  50 us
    all_gather x1, waiting for transfers between devices, local(): handoff = lax.all_gather(handoff, 'dp', axis=0, tiled=True)  33.9 us
    all_to_all x1, blocking collectives, local(): lax.all_to_all(summed, 'dp', split_axis=0, concat_axis=0, tiled=True)  19.1 us
    dot_general x2, matrix products, transposed_product(): lax.dot_general(left, right, (((1,), (1,)), ((), ())), preferred_element_...  13.6 us
    all_to_all x1, blocking collectives, local(): lax.all_to_all(handoff, 'tensor', split_axis=1, concat_axis=0, tiled=True)  11 us
    all_to_all x1, blocking collectives, local(): lax.all_to_all(summed, 'tensor', split_axis=1, concat_axis=0, tiled=True)  10.6 us
    all_gather x1, blocking collectives, local(): target = lax.all_gather(target, 'dp', axis=0)  10.4 us
  transfers between devices with their start and end apart: 7, of which 6 were waited for; matrix products, arithmetic and copies ran while one was open for 5% of the time, Pallas kernels for 0%

profile of v1, /device:TPU:0, one launch (start us, length us, event | category | flops | bytes accessed | tf_op | source)
XLA Modules:
  0.0 327.6 jit_solution(7552467505674855836)
XLA Ops:
  6.5 0.0 copy-start
  6.5 0.0 all-gather.4.cloned.1.call-start
  6.5 0.8 compare_select_fusion
  7.3 0.7 compare_and_fusion
  8.0 2.8 gather_fusion
  10.8 3.6 %gather_fusion.1 = bf16[128,2048]{1,0:T(8,128)(2,1)} fusion(bf16[256,2048]{1,0:T(8,128)(2,1)} %param.15, s32[1024]{0:T(1024)S(1)} %pad_clamp_fusion), kind=kCustom, calls=%fused_computation.1.clone | custom fusion | bytes 1049088 | tf_op jit(solution)/shard_map/jit(_take)/gather | solution.py:55
  14.4 3.6 %gather_fusion.2 = bf16[128,2048]{1,0:T(8,128)(2,1)} fusion(bf16[256,2048]{1,0:T(8,128)(2,1)} %param.12, s32[1024]{0:T(1024)S(1)} %pad_clamp_fusion), kind=kCustom, calls=%fused_computation.2.clone | custom fusion | bytes 1049088 | tf_op jit(solution)/shard_map/jit(_take)/gather | solution.py:54
  18.0 2.5 broadcast_select_fusion.2
  20.5 0.0 all-gather.4.cloned.1.call-update
  20.5 0.0 reduce-scatter.7.cloned.1.call-start
  20.6 50.0 %all-gather.4.cloned.1.call-done = bf16[1024,2048]{1,0:T(8,128)(2,1)} async-done(((bf16[128,2048]{1,0:T(8,128)(2,1)}), bf16[1024,2048]{1,0:T(8,128)(2,1)}) %all-gather.4.cloned.1.call-update) | async-done | bytes 4194320 | tf_op jit(solution)/shard_map/all_gather | solution.py:54
  70.5 8.0 %convolution_convert_fusion = bf16[1024,1024]{1,0:T(8,128)(2,1)S(1)} fusion(bf16[1024,2048]{1,0:T(8,128)(2,1)} %all-gather.4.cloned.1.call-done, bf16[1024,2048]{1,0:T(8,128)(2,1)} %param.13), kind=kOutput, calls=%fused_computation.3 | convolution fusion | flops 4296015872 | bytes 10485760 | tf_op jit(solution)/shard_map/dot_general | solution.py:17
  78.5 2.5 copy.32
  81.0 0.0 copy-start.1
  81.0 0.0 reduce-scatter.7.cloned.1.call-update
  81.0 3.7 %all-to-all-start.1 = ((bf16[4,32,2048]{2,1,0:T(8,128)(2,1)}), bf16[4,32,2048]{2,1,0:T(8,128)(2,1)S(1)}, u32[]{:S(2)}, u32[]{:S(2)}) async-start(bf16[4,32,2048]{2,1,0:T(8,128)(2,1)} %bitcast.71), calls=%async_computation.1 | async-start | bytes 1048576 | tf_op jit(solution)/shard_map/all_to_all | solution.py:57
  84.7 32.9 %reduce-scatter.7.cloned.1.call-done = bf16[8,1,32,1024]{3,0,2,1:T(8,128)(2,1)} async-done(((bf16[8,4,32,1024]{3,0,2,1:T(8,128)(2,1)}), bf16[8,1,32,1024]{3,0,2,1:T(8,128)(2,1)}) %reduce-scatter.7.cloned.1.call-update) | async-done | bytes 524304
  117.6 2.1 copy.33
  119.8 0.0 all-to-all-done.1
  119.8 4.6 %all-to-all-start.2 = ((bf16[8,32,1024]{2,1,0:T(8,128)(2,1)}), bf16[8,32,1024]{2,1,0:T(8,128)(2,1)}, u32[]{:S(2)}, u32[]{:S(2)}) async-start(bf16[8,32,1024]{2,1,0:T(8,128)(2,1)} %copy.33), calls=%async_computation.2 | async-start | bytes 1048576 | tf_op jit(solution)/shard_map/all_to_all | solution.py:67
  124.4 0.0 copy-done.1
  124.4 8.1 %all_gather.14 = f32[8192]{0:T(1024)S(1)} all-gather(f32[2048]{0:T(1024)S(1)} %copy-done.1), channel_id=1, replica_groups=mesh['dp'=8,'tensor'=4] {'tensor'}, dimensions={0}, use_global_device_ids=true | all-gather | bytes 40960 | tf_op jit(solution)/shard_map/all_gather | solution.py:60
  132.5 0.1 convert_bitcast_fusion
  132.6 1.7 copy.36
  134.3 2.6 reshape.92
  136.9 0.2 fusion.3
  137.2 2.7 all-to-all-done.2
  139.8 4.1 %all-to-all-start = ((bf16[4,32,2048]{2,1,0:T(8,128)(2,1)}), bf16[4,32,2048]{2,1,0:T(8,128)(2,1)}, u32[]{:S(2)}, u32[]{:S(2)}) async-start(bf16[4,32,2048]{2,1,0:T(8,128)(2,1)} %bitcast.70), calls=%async_computation | async-start | bytes 1048576 | tf_op jit(solution)/shard_map/all_to_all | solution.py:58
  144.0 0.2 all-gather.6.cloned.1.call-start
  144.2 2.4 convert_bitcast_fusion.1
  146.6 2.8 reshape.91
  149.3 0.0 copy-start.2
  149.3 1.9 fusion.2
  151.3 0.9 all-to-all-done
  152.1 2.1 fusion.6
  154.2 11.0 %all_to_all.65 = bf16[32,4,2048]{2,0,1:T(8,128)(2,1)} all-to-all(bf16[32,4,2048]{2,0,1:T(8,128)(2,1)S(1)} %fusion.6), channel_id=1, replica_groups=mesh['dp'=8,'tensor'=4] {'tensor'}, dimensions={1} | all-to-all | bytes 1048576 | tf_op jit(solution)/shard_map/all_to_all | solution.py:80
  165.3 0.0 all-gather.6.cloned.1.call-update
  165.3 0.0 all-reduce.4.cloned.1.call-start
  166.0 0.0 copy-done.2
  166.0 0.1 fusion.17
  166.1 0.2 reduce_window_sum.11
  166.3 0.2 select_reduce_fusion
  166.5 10.4 %all-gather = s32[8,1,128]{2,1,0:T(1,128)S(1)} all-gather(s32[1,1,128]{2,1,0:T(1,128)S(1)} %fusion.19), channel_id=1, replica_groups=mesh['dp'=8,'tensor'=4] {'dp'}, dimensions={0}, use_global_device_ids=true | all-gather | bytes 4608 | tf_op jit(solution)/shard_map/all_gather | solution.py:62
  176.9 33.9 %all-gather.6.cloned.1.call-done = bf16[1024,2048]{1,0:T(8,128)(2,1)} async-done(((bf16[128,2048]{1,0:T(8,128)(2,1)}), bf16[1024,2048]{1,0:T(8,128)(2,1)}) %all-gather.6.cloned.1.call-update) | async-done | bytes 4194320 | tf_op jit(solution)/shard_map/all_gather | solution.py:81
  210.7 0.0 copy-done
  210.7 5.6 %convolution_convert_fusion.2 = bf16[1024,640]{1,0:T(8,128)(2,1)S(1)} fusion(bf16[1024,2048]{1,0:T(8,128)(2,1)} %all-gather.6.cloned.1.call-done, bf16[640,2048]{1,0:T(8,128)(2,1)S(1)} %copy-done), kind=kOutput, calls=%fused_computation.9 | convolution fusion | flops 2685009920 | bytes 8126464 | tf_op jit(solution)/shard_map/dot_general | solution.py:17
  216.4 0.7 convolution_convert_fusion.1
  217.0 0.0 copy-start.3
  217.0 1.5 copy.37
  218.6 0.0 all-reduce.4.cloned.1.call-update
  218.6 0.0 copy-done.3
  218.6 0.6 dynamic-slice
  219.2 65.8 %all-reduce.4.cloned.1.call-done = bf16[8,4,48,640]{3,2,1,0:T(8,128)(2,1)} async-done(((bf16[8,4,48,640]{3,2,1,0:T(8,128)(2,1)}), bf16[8,4,48,640]{3,2,1,0:T(8,128)(2,1)}) %all-reduce.4.cloned.1.call-update) | async-done | bytes 1966096
  284.9 1.7 dynamic-slice_bitcast_fusion
  286.7 19.1 %all_to_all.66 = bf16[8,48,640]{2,1,0:T(8,128)(2,1)S(1)} all-to-all(bf16[8,48,640]{2,1,0:T(8,128)(2,1)S(1)} %dynamic-slice_bitcast_fusion), channel_id=1, replica_groups=mesh['dp'=8,'tensor'=4] {'dp'}, dimensions={0} | all-to-all | bytes 983040 | tf_op jit(solution)/shard_map/all_to_all | solution.py:93
  305.7 0.1 copy.38
  305.8 1.1 all_to_all.57
  306.9 1.1 copy.39
  308.0 10.6 %all_to_all.67 = bf16[48,4,1280]{2,0,1:T(8,128)(2,1)S(1)} all-to-all(bf16[48,4,1280]{2,0,1:T(8,128)(2,1)S(1)} %copy.39), channel_id=1, replica_groups=mesh['dp'=8,'tensor'=4] {'tensor'}, dimensions={1} | all-to-all | bytes 983040 | tf_op jit(solution)/shard_map/all_to_all | solution.py:95
  318.6 2.4 fusion.12
  (6 shorter events, 0.1 us)
Async XLA Ops:
  6.5 204.2 %copy-start = (bf16[640,2048]{1,0:T(8,128)(2,1)S(1)}, bf16[640,2048]{1,0:T(8,128)(2,1)}, u32[]{:S(2)}) copy-start(bf16[640,2048]{1,0:T(8,128)(2,1)} %param.20) | copy-start | bytes 7864324
  6.5 64.0 %all-gather.4.cloned.1.call-start = ((), (), s32[]{:S(2)}) async-start(), calls=%async_computation.7 | async-start | bytes 4718592 | tf_op jit(solution)/shard_map/all_gather | solution.py:54
  20.5 97.1 %reduce-scatter.7.cloned.1.call-start = ((), (), s32[]{:S(2)}) async-start(), calls=%async_computation.10 | async-start | bytes 2621440
  81.0 43.4 %copy-start.1 = (f32[2048]{0:T(1024)S(1)}, f32[2048]{0:T(1024)}, u32[]{:S(2)}) copy-start(f32[2048]{0:T(1024)} %param.16) | copy-start | bytes 24580
  81.0 38.7 %all-to-all-start.1 = ((bf16[4,32,2048]{2,1,0:T(8,128)(2,1)}), bf16[4,32,2048]{2,1,0:T(8,128)(2,1)S(1)}, u32[]{:S(2)}, u32[]{:S(2)}) async-start(bf16[4,32,2048]{2,1,0:T(8,128)(2,1)} %bitcast.71), calls=%async_computation.1 | async-start | bytes 1048576 | tf_op jit(solution)/shard_map/all_to_all | solution.py:57
  119.8 20.1 %all-to-all-start.2 = ((bf16[8,32,1024]{2,1,0:T(8,128)(2,1)}), bf16[8,32,1024]{2,1,0:T(8,128)(2,1)}, u32[]{:S(2)}, u32[]{:S(2)}) async-start(bf16[8,32,1024]{2,1,0:T(8,128)(2,1)} %copy.33), calls=%async_computation.2 | async-start | bytes 1048576 | tf_op jit(solution)/shard_map/all_to_all | solution.py:67
  139.8 12.3 %all-to-all-start = ((bf16[4,32,2048]{2,1,0:T(8,128)(2,1)}), bf16[4,32,2048]{2,1,0:T(8,128)(2,1)}, u32[]{:S(2)}, u32[]{:S(2)}) async-start(bf16[4,32,2048]{2,1,0:T(8,128)(2,1)} %bitcast.70), calls=%async_computation | async-start | bytes 1048576 | tf_op jit(solution)/shard_map/all_to_all | solution.py:58
  144.0 66.7 %all-gather.6.cloned.1.call-start = ((), (), s32[]{:S(2)}) async-start(), calls=%async_computation.8 | async-start | bytes 4718592 | tf_op jit(solution)/shard_map/all_gather | solution.py:81
  149.3 16.7 %copy-start.2 = (s32[1,128]{1,0:T(1,128)S(1)}, s32[1,128]{1,0:T(1,128)}, u32[]{:S(2)}) copy-start(s32[1,128]{1,0:T(1,128)} %param.19) | copy-start | bytes 1540
  165.3 119.7 %all-reduce.4.cloned.1.call-start = ((), (), s32[]{:S(2)}) async-start(), calls=%async_computation.9 | async-start | bytes 3932160
  217.0 1.6 copy-start.3
Sparse Core Ops, SparseCore 0:
  20.6 49.8 all-gather.3
  81.2 36.4 reduce-scatter.6
  165.4 45.2 all-gather.5
  218.7 66.1 all-reduce.3

commit v2 on v1

--- a/solution.py
+++ b/solution.py
@@ -1,6 +1,10 @@
+import functools
+
 import jax
 import jax.numpy as jnp
 from jax import lax
+from jax.experimental import pallas as pl
+from jax.experimental.pallas import tpu as pltpu
 from jax.sharding import PartitionSpec as P
 
 NORM_EPS = 1e-06
@@ -96,6 +100,499 @@
     return hidden_grad.astype(jnp.float32) * gelu_slope(merge_pre)
 
 
+Z = 4
+CORES = 2
+PARTS = 4
+UNIT = 16
+UNITS = 3
+MESH = pl.DeviceIdType.MESH
+BF16 = jnp.bfloat16
+F32 = jnp.float32
+
+
+def stage_order(z, step):
+    near = jnp.where(z >= 2, Z - 1 - z, z)
+    at = jnp.where((near == 1) & (step < 2), 1 - step, step)
+    return jnp.where(z >= 2, Z - 1 - at, at)
+
+
+def remote(src, dst, send, recv, device):
+    return pltpu.make_async_remote_copy(
+        src_ref=src, dst_ref=dst, send_sem=send, recv_sem=recv, device_id=device, device_id_type=MESH
+    )
+
+
+def fused_kernel(
+    capacity,
+    gq, pos, count, dest, gain, wq_hbm, em_hbm, gr_hbm, wm_hbm, mp_hbm,
+    out,
+    wq, em, gr, wm, mp, slope,
+    x, part, part_in, sums, grads,
+    x_send, x_in, r_send, r_in, gains, rows_at,
+    h_send, h, q, q_in, u, w, f,
+    local_sem, x_s, x_r, part_s, part_r, sums_s, grads_r,
+    em_s, em_r, gr_s, gr_r, gain_s, gain_r, at_s, at_r,
+    hs_s, h_s, h_r, q_s, q_r, u_s, w_r, w_s, f_r,
+):
+    s = lax.axis_index("dp")
+    t = lax.axis_index("tensor")
+    z = s // CORES
+    c = s % CORES
+    groups = Z * CORES
+    sib = z * CORES + 1 - c
+    sibling = (sib, t)
+    tokens = gq.shape[0]
+    image_count = pos.shape[1]
+    rows = image_count // PARTS
+    block = wq.shape[0]
+    width = block * groups
+    hidden = wm.shape[0]
+    middle = (z == 1) | (z == 2)
+
+    loads = [
+        pltpu.make_async_copy(src, dst, local_sem.at[i])
+        for i, (src, dst) in enumerate(
+            ((em_hbm, em), (gr_hbm, gr), (wq_hbm, wq), (mp_hbm, mp), (wm_hbm, wm))
+        )
+    ]
+    for load in loads:
+        load.start()
+
+    barrier = pltpu.get_barrier_semaphore()
+    for k in range(1, groups):
+        pl.semaphore_signal(barrier, inc=1, device_id=((s + k) % groups, t), device_id_type=MESH)
+    for k in range(1, PARTS):
+        pl.semaphore_signal(barrier, inc=1, device_id=(s, (t + k) % PARTS), device_id_type=MESH)
+
+    hot = (lax.broadcasted_iota(jnp.int32, (tokens, image_count), 0) == pos[...]).astype(F32).astype(BF16)
+
+    def pick(ref):
+        return lax.dot_general(
+            hot, ref[...], (((0,), (0,)), ((), ())), preferred_element_type=F32
+        ).astype(BF16)
+
+    x[pl.ds(s, 1)] = pick(gq)[None]
+    pl.semaphore_wait(barrier, groups - 1 + PARTS - 1)
+
+    def to_right(b, d):
+        return remote(x.at[b], x.at[b], x_s.at[b, 0], x_r.at[b], (s + CORES, t))
+
+    def to_left(b, d):
+        return remote(x.at[b], x.at[b], x_s.at[b, 1], x_r.at[b], (s - CORES, t))
+
+    def to_sibling(b, d):
+        return remote(x.at[b], x.at[b], x_s.at[b, 2], x_r.at[b], sibling)
+
+    def h_right(b, d):
+        return remote(h.at[b, d], h.at[b, d], h_s.at[b, d, 0], h_r.at[b, d], (s + CORES, t))
+
+    def h_left(b, d):
+        return remote(h.at[b, d], h.at[b, d], h_s.at[b, d, 1], h_r.at[b, d], (s - CORES, t))
+
+    def h_sibling(b, d):
+        return remote(h.at[b, d], h.at[b, d], h_s.at[b, d, 2], h_r.at[b, d], sibling)
+
+    def spread(act, kinds, zz, d):
+        b = zz * CORES + c
+        right, left, side = kinds
+
+        @pl.when((zz <= z) & (z < Z - 1))
+        def _():
+            act(right(b, d))
+
+        @pl.when((zz >= z) & (z > 0))
+        def _():
+            act(left(b, d))
+
+        act(side(b, d))
+
+    def start(copy):
+        copy.start()
+
+    def sent(copy):
+        copy.wait_send()
+
+    x_kinds = (to_right, to_left, to_sibling)
+    h_kinds = (h_right, h_left, h_sibling)
+    spread(start, x_kinds, z, 0)
+
+    def peer(k):
+        return (t + k) % PARTS
+
+    gains[pl.ds(t, 1)] = jnp.broadcast_to(gain[...], (1, 8, gain.shape[1]))
+    loads[0].wait()
+    x_send[...] = pick(em).reshape(x_send.shape)
+    loads[1].wait()
+    r_send[...] = pick(gr).reshape(r_send.shape)
+
+    def row_copies(k):
+        p = peer(k)
+        return (
+            remote(x_send.at[p], x_in.at[t], em_s.at[k], em_r.at[t], (s, p)),
+            remote(r_send.at[p], r_in.at[t], gr_s.at[k], gr_r.at[t], (s, p)),
+            remote(gains.at[t], gains.at[t], gain_s.at[k], gain_r.at[t], (s, p)),
+        )
+
+    for k in range(1, PARTS):
+        for copy in row_copies(k):
+            copy.start()
+    x_in[pl.ds(t, 1)] = x_send[pl.ds(t, 1)]
+    r_in[pl.ds(t, 1)] = r_send[pl.ds(t, 1)]
+
+    lane = lax.broadcasted_iota(jnp.int32, (groups, image_count), 1)
+    hot_dest = (dest[...] == lax.broadcasted_iota(jnp.int32, (groups, image_count), 0)) & (lane < count[0])
+    hot_dest = hot_dest.astype(F32)
+    before = (
+        lax.broadcasted_iota(jnp.int32, (image_count, image_count), 0)
+        < lax.broadcasted_iota(jnp.int32, (image_count, image_count), 1)
+    ).astype(F32)
+    earlier = jnp.dot(hot_dest, before, preferred_element_type=F32)
+    slot = jnp.sum(earlier * hot_dest, axis=0, keepdims=True).astype(jnp.int32)
+    spot = c * capacity + slot
+    at = lax.shift_right_logical(spot, 4) * (groups * UNIT) + dest[...] * UNIT + (spot & (UNIT - 1))
+    at = jnp.where(lane[:1] < count[0], at, -1)
+    rows_at[pl.ds(s, 1)] = jnp.broadcast_to(at, (1, 8, image_count))
+
+    def at_copy(k):
+        return remote(rows_at.at[s], rows_at.at[s], at_s.at[k], at_r.at[s], ((s + k) % groups, t))
+
+    for k in range(1, groups):
+        at_copy(k).start()
+
+    def part_copy(zz, k):
+        p = peer(k)
+        return remote(part.at[zz, p], part_in.at[zz, t], part_s.at[zz, k], part_r.at[zz, t], (s, p))
+
+    def sums_copy(zz, cc):
+        return remote(
+            sums.at[zz, cc], grads.at[s], sums_s.at[zz, cc], grads_r.at[s], (zz * CORES + cc, t)
+        )
+
+    def arrived(ref, sem):
+        remote(ref, ref, x_s.at[0, 0], sem, sibling).wait_recv()
+
+    def add_parts(zz):
+        total = part[zz, t].astype(F32)
+        for k in range(1, PARTS):
+            p = peer(k)
+            arrived(part_in.at[zz, p], part_r.at[zz, p])
+            total += part_in[zz, p].astype(F32)
+        sums[pl.ds(zz, 1)] = total.astype(BF16)[None]
+        for cc in range(CORES):
+            own = (zz == z) & (c == cc)
+
+            @pl.when(jnp.logical_not(own))
+            def _():
+                sums_copy(zz, cc).start()
+
+            @pl.when(own)
+            def _():
+                grads[pl.ds(s, 1)] = sums[zz, cc][None]
+
+    loads[2].wait()
+
+    def pass_on(zz):
+        b = zz * CORES + c
+        arrived(x.at[b], x_r.at[b])
+        spread(start, x_kinds, zz, 0)
+
+    def first_step(step, carry):
+        zz = stage_order(z, step)
+
+        @pl.when((step == 1) | (step == 3) | ((step == 2) & jnp.logical_not(middle)))
+        def _():
+            pass_on(zz)
+
+        @pl.when((step == 1) & middle)
+        def _():
+            pass_on(stage_order(z, 2))
+
+        b = zz * CORES + 1 - c
+        arrived(x.at[b], x_r.at[b])
+        left = x[pl.ds(zz * CORES, CORES)].reshape(CORES * image_count, -1)
+        tile = 256
+        for n in range(0, block, tile):
+            piece = transposed_product(left, wq[n:n + tile]).astype(BF16)
+            piece = piece.reshape(CORES, PARTS, rows, tile)
+            for p in range(PARTS):
+                part[pl.ds(zz, 1), p, :, :, n:n + tile] = piece[:, p][None]
+        for k in range(1, PARTS):
+            part_copy(zz, k).start()
+
+        @pl.when(step == 0)
+        def _():
+            loads[3].wait()
+
+            def some_rows(i, carry):
+                span = pl.ds(pl.multiple_of(i * UNIT, UNIT), UNIT)
+                slope[span] = gelu_slope(mp[span])
+                return carry
+
+            lax.fori_loop(0, mp.shape[0] // UNIT, some_rows, 0)
+
+        @pl.when(step > 0)
+        def _():
+            add_parts(stage_order(z, step - 1))
+
+        return carry
+
+    lax.fori_loop(0, Z, first_step, 0)
+    for k in range(1, PARTS):
+        p = peer(k)
+        arrived(x_in.at[p], em_r.at[p])
+        arrived(r_in.at[p], gr_r.at[p])
+        arrived(gains.at[p], gain_r.at[p])
+    squares = jnp.zeros((rows, 1), F32)
+    for p in range(PARTS):
+        value = x_in[p].astype(F32)
+        squares += jnp.sum(value * value, axis=1, keepdims=True)
+    inverse = lax.rsqrt(squares / width + NORM_EPS)
+    add_parts(stage_order(z, Z - 1))
+
+    for k in range(1, groups):
+        b = (s + k) % groups
+        arrived(grads.at[b], grads_r.at[b])
+
+    def scaled_block(b):
+        lo = (b % 2) * block
+        return gains[b // 2, 0:1, lo:lo + block] * grads[b].astype(F32)
+
+    inner = jnp.zeros((rows, 1), F32)
+    for b in range(groups):
+        lo = (b % 2) * block
+        value = x_in[b // 2, :, lo:lo + block].astype(F32)
+        inner += jnp.sum(scaled_block(b) * value, axis=1, keepdims=True)
+    back = inverse * inverse * inverse * inner / width
+    for b in range(groups):
+        lo = (b % 2) * block
+        value = x_in[b // 2, :, lo:lo + block].astype(F32)
+        residual = r_in[b // 2, :, lo:lo + block].astype(F32)
+        result = residual + inverse * scaled_block(b) - value * back
+        h_send[b // 2, :, lo:lo + block] = result.astype(BF16)
+
+    def hand_copy(k):
+        p = peer(k)
+        return remote(h_send.at[p], h.at[s, t], hs_s.at[k], h_r.at[s, t], (s, p))
+
+    for k in range(1, PARTS):
+        hand_copy(k).start()
+    h[pl.ds(s, 1), pl.ds(t, 1)] = h_send[pl.ds(t, 1)][None]
+    for k in range(PARTS):
+        d = peer(k)
+        if k:
+            arrived(h.at[s, d], h_r.at[s, d])
+        spread(start, h_kinds, z, d)
+
+    for k in range(1, groups):
+        b = (s + k) % groups
+        arrived(rows_at.at[b], at_r.at[b])
+    loads[4].wait()
+
+    def unit_of(p, zz):
+        return (p + zz) % PARTS
+
+    def q_copy(zz, k):
+        p = peer(k)
+        return remote(
+            q.at[zz, unit_of(p, zz)], q_in.at[zz, t], q_s.at[zz, k], q_r.at[zz, t], (s, p)
+        )
+
+    def u_copy(zz, r):
+        return remote(u.at[zz, r], w.at[s, zz], u_s.at[zz, r], w_r.at[s, zz], (r, t))
+
+    def add_units(zz):
+        @pl.when(unit_of(t, zz) < UNITS)
+        def _():
+            total = q[zz, unit_of(t, zz)].astype(F32)
+            for k in range(1, PARTS):
+                p = peer(k)
+                arrived(q_in.at[zz, p], q_r.at[zz, p])
+                total += q_in[zz, p].astype(F32)
+            u[pl.ds(zz, 1)] = total.astype(BF16)[None]
+            for k in range(1, groups):
+                u_copy(zz, (s + k) % groups).start()
+            w[pl.ds(s, 1), pl.ds(zz, 1)] = u[zz, s][None, None]
+
+    def h_pass(zz, k):
+        b = zz * CORES + c
+        d = peer(k)
+        arrived(h.at[b, d], h_r.at[b, d])
+        spread(start, h_kinds, zz, d)
+
+    def second_step(step, carry):
+        zz = stage_order(z, step)
+        for k in range(PARTS):
+            @pl.when((step == 1) | (step == 3) | ((step == 2) & jnp.logical_not(middle)))
+            def _():
+                h_pass(zz, k)
+
+            @pl.when((step == 1) & middle)
+            def _():
+                h_pass(stage_order(z, 2), k)
+
+        b = zz * CORES + 1 - c
+        for k in range(PARTS):
+            d = peer(k)
+            arrived(h.at[b, d], h_r.at[b, d])
+        left = h[pl.ds(zz * CORES, CORES)].reshape(CORES * image_count, -1)
+        spots = jnp.concatenate([rows_at[zz * CORES, 0:1], rows_at[zz * CORES + 1, 0:1]], axis=1)
+        placed_rows = UNITS * groups * UNIT
+        place = lax.broadcasted_iota(jnp.int32, (placed_rows, CORES * image_count), 0) == spots
+        place = place.astype(F32).astype(BF16)
+        lo = 0
+        while lo < hidden:
+            hi = min(lo + 256, hidden)
+            piece = transposed_product(left, wm[lo:hi]).astype(BF16)
+            piece = jnp.dot(place, piece, preferred_element_type=F32).astype(BF16)
+            q[pl.ds(zz, 1), :, :, :, lo:hi] = piece.reshape(1, UNITS, groups, UNIT, hi - lo)
+            lo = hi
+        for k in range(1, PARTS):
+            @pl.when(unit_of(peer(k), zz) < UNITS)
+            def _():
+                q_copy(zz, k).start()
+
+        @pl.when(step > 0)
+        def _():
+            add_units(stage_order(z, step - 1))
+
+        return carry
+
+    lax.fori_loop(0, Z, second_step, 0)
+    add_units(stage_order(z, Z - 1))
+
+    def f_copy(b, zz):
+        unit = zz * UNITS + unit_of(t, zz)
+        return remote(w.at[b, zz], f.at[unit, b % 2], w_s.at[b, zz], f_r.at[unit, b % 2], (s, b // 2))
+
+    def hand_out(i, carry):
+        step, k = i // groups, i % groups
+        b = (s + k) % groups
+        zz = stage_order(b // CORES, step)
+
+        @pl.when(unit_of(t, zz) < UNITS)
+        def _():
+            @pl.when(b != s)
+            def _():
+                arrived(w.at[b, zz], w_r.at[b, zz])
+
+            @pl.when(b // 2 != t)
+            def _():
+                f_copy(b, zz).start()
+
+            @pl.when(b // 2 == t)
+            def _():
+                unit = zz * UNITS + unit_of(t, zz)
+                f[pl.ds(unit, 1), pl.ds(b % 2, 1)] = w[b, zz][None, None]
+
+        return carry
+
+    lax.fori_loop(0, Z * groups, hand_out, 0)
+
+    def finish(unit, carry):
+        zz, k = unit // UNITS, unit % UNITS
+        span = pl.ds(pl.multiple_of(unit * UNIT, UNIT), UNIT)
+        for half in range(2):
+            @pl.when((k + PARTS - zz) % PARTS != t)
+            def _():
+                arrived(f.at[unit, half], f_r.at[unit, half])
+
+            columns = slice(half * hidden, (half + 1) * hidden)
+            out[span, columns] = f[unit, half].astype(F32) * slope[span, columns]
+        return carry
+
+    lax.fori_loop(0, Z * UNITS, finish, 0)
+
+    for k in range(1, PARTS):
+        for copy in row_copies(k):
+            sent(copy)
+        sent(hand_copy(k))
+    for k in range(1, groups):
+        sent(at_copy(k))
+
+    def all_sent(zz, carry):
+        spread(sent, x_kinds, zz, 0)
+        for d in range(PARTS):
+            spread(sent, h_kinds, zz, d)
+        for k in range(1, PARTS):
+            sent(part_copy(zz, k))
+
+            @pl.when(unit_of(peer(k), zz) < UNITS)
+            def _():
+                sent(q_copy(zz, k))
+
+        for cc in range(CORES):
+            @pl.when((zz != z) | (c != cc))
+            def _():
+                sent(sums_copy(zz, cc))
+
+        @pl.when(unit_of(t, zz) < UNITS)
+        def _():
+            for k in range(1, groups):
+                sent(u_copy(zz, (s + k) % groups))
+            for b in range(groups):
+                @pl.when(b // 2 != t)
+                def _():
+                    sent(f_copy(b, zz))
+
+        return carry
+
+    lax.fori_loop(0, Z, all_sent, 0)
+
+
+def fused(grad_query, query_weight, grad_resid, embeds, norm_gain, img_pos, img_count, img_dest, merge_weight, merge_pre):
+    groups = Z * CORES
+    capacity = merge_pre.shape[0] // groups
+    image_count = img_pos.shape[1]
+    rows = image_count // PARTS
+    block, columns = query_weight.shape
+    hidden = merge_weight.shape[0]
+    vmem = pltpu.VMEM
+    dma = pltpu.SemaphoreType.DMA
+    in_vmem = pl.BlockSpec(memory_space=pltpu.VMEM)
+    anywhere = pl.BlockSpec(memory_space=pl.ANY)
+    scratch = [
+        vmem(query_weight.shape, BF16), vmem(embeds.shape, BF16), vmem(grad_resid.shape, BF16),
+        vmem(merge_weight.shape, BF16), vmem(merge_pre.shape, BF16), vmem(merge_pre.shape, F32),
+        vmem((groups, image_count, columns), BF16),
+        vmem((Z, PARTS, CORES, rows, block), BF16), vmem((Z, PARTS, CORES, rows, block), BF16),
+        vmem((Z, CORES, rows, block), BF16), vmem((groups, rows, block), BF16),
+        vmem((PARTS, rows, columns), BF16), vmem((PARTS, rows, columns), BF16),
+        vmem((PARTS, rows, columns), BF16), vmem((PARTS, rows, columns), BF16),
+        vmem((PARTS, 8, columns), F32), vmem((groups, 8, image_count), jnp.int32),
+        vmem((PARTS, rows, columns), BF16), vmem((groups, PARTS, rows, columns), BF16),
+        vmem((Z, UNITS, groups, UNIT, hidden), BF16), vmem((Z, PARTS, groups, UNIT, hidden), BF16),
+        vmem((Z, groups, UNIT, hidden), BF16), vmem((groups, Z, UNIT, hidden), BF16),
+        vmem((Z * UNITS, 2, UNIT, hidden), BF16),
+        dma((5,)), dma((groups, 3)), dma((groups,)), dma((Z, PARTS)), dma((Z, PARTS)),
+        dma((Z, CORES)), dma((groups,)),
+        dma((PARTS,)), dma((PARTS,)), dma((PARTS,)), dma((PARTS,)), dma((PARTS,)), dma((PARTS,)),
+        dma((groups,)), dma((groups,)),
+        dma((PARTS,)), dma((groups, PARTS, 3)), dma((groups, PARTS)), dma((Z, PARTS)), dma((Z, PARTS)),
+        dma((Z, groups)), dma((groups, Z)), dma((groups, Z)), dma((Z * UNITS, 2)),
+    ]
+    return pl.pallas_call(
+        functools.partial(fused_kernel, capacity),
+        out_shape=jax.ShapeDtypeStruct(merge_pre.shape, F32),
+        in_specs=[
+            in_vmem, in_vmem, pl.BlockSpec(memory_space=pltpu.SMEM), in_vmem, in_vmem,
+            anywhere, anywhere, anywhere, anywhere, anywhere,
+        ],
+        out_specs=in_vmem,
+        scratch_shapes=scratch,
+        compiler_params=pltpu.CompilerParams(
+            collective_id=0, has_side_effects=True, vmem_limit_bytes=56 * 1024 * 1024
+        ),
+        cost_estimate=pl.CostEstimate(
+            flops=4 * groups * image_count * columns * (block + hidden),
+            bytes_accessed=16 * 1024 * 1024,
+            transcendentals=merge_pre.size,
+        ),
+    )(
+        grad_query, img_pos, img_count, img_dest, norm_gain.reshape(1, -1),
+        query_weight, embeds, grad_resid, merge_weight, merge_pre,
+    )
+
+
 def solution(mesh):
     in_specs = (
         P("dp", "tensor"),
@@ -110,4 +607,6 @@
         P("dp", "tensor"),
     )
     out_specs = P("dp", "tensor")
-    return jax.shard_map(local, mesh=mesh, in_specs=in_specs, out_specs=out_specs, check_vma=False)
+    known = mesh.shape["dp"] == Z * CORES and mesh.shape["tensor"] == PARTS
+    body = fused if known else local
+    return jax.shard_map(body, mesh=mesh, in_specs=in_specs, out_specs=out_specs, check_vma=False)

time: 329 us -> 141 us (0.43)
  waiting for transfers between devices: 186 us -> 0 us
  Pallas kernels: 0 us -> 138 us
  blocking collectives: 59.2 us -> 0 us
  local copies, waits for them, and re-layouts: 27.9 us -> 2.21 us
  matrix products: 14.3 us -> 0 us
  other arithmetic: 13.6 us -> 0 us
  between operations: 13.9 us -> 0.66 us
  starting transfers between devices: 12.7 us -> 0 us
    pallas_call x0 -> x1, Pallas kernels: none -> 138 us  [fused(): pl.pallas_call(functools.partial(fused_kernel, capacity), out_shape=jax.S...]
    unnamed x6 -> x0, waiting for transfers between devices: 98.7 us -> none
    all_gather x2 -> x0, waiting for transfers between devices: 83.8 us -> none  [the longest x1 50 us: local(): lax.all_gather(jnp.take(grad_query, positions, axis=0), 'dp', axis=0, til...]
    all_to_all x3 -> x0, blocking collectives: 40.7 us -> none  [the longest x1 19.1 us: local(): lax.all_to_all(summed, 'dp', split_axis=0, concat_axis=0, tiled=True)]
    all_gather x2 -> x0, blocking collectives: 18.5 us -> none  [the longest x1 10.4 us: local(): target = lax.all_gather(target, 'dp', axis=0)]
    dot_general x3 -> x0, matrix products: 14.3 us -> none  [the longest x2 13.6 us: transposed_product(): lax.dot_general(left, right, (((1,), (1,)), ((), ())), preferred_element_...]
    all_to_all x3 -> x0, starting transfers between devices: 12.4 us -> none  [the longest x1 4.61 us: local(): lax.all_to_all(summed, 'dp', split_axis=0, concat_axis=0, tiled=True)]
    gather x3 -> x0, local copies, waits for them, and re-layouts: 10 us -> none  [the longest x1 3.6 us: local(): jnp.take(grad_query, positions, axis=0)]
  transfers between devices with their start and end apart: 7 -> 0, of which waited for: 6 -> 0; matrix products, arithmetic and copies ran while one was open for 5% -> 0% of each run, Pallas kernels for 0% -> 0%
where the time goes in v2:
time: 141 us
  Pallas kernels  138 us (98%)
  local copies, waits for them, and re-layouts  2.21 us (2%)
    pallas_call x1, Pallas kernels, fused(): pl.pallas_call(functools.partial(fused_kernel, capacity), out_shape=jax.S...  138 us

profile of v2, /device:TPU:0, one launch (start us, length us, event | category | flops | bytes accessed | tf_op | source)
XLA Modules:
  0.0 141.1 jit_solution(7548217514446388584)
XLA Ops:
  0.7 138.2 %shard_map.100 = f32[192,1280]{1,0:T(8,128)} custom-call(bf16[256,2048]{1,0:T(8,128)(2,1)} %gq.1, s32[1,128]{1,0:T(1,128)} %pos.1, s32[1]{0:T(128)S(6)} %copy.12.count, s32[1,128]{1,0:T(1,128)} %dest.1, f32[1,2048]{1,0:T(1,128)} %bitcast.1, bf16[1024,2048]{1,0:T(8,128)(2,1)} %wq_hbm.1, bf16[256,2048]{1,0:T(8,128)(2,1)} %em_hbm.1, bf16[256,2048]{1,0:T(8,128)(2,1)} %gr_hbm.1, ...), custom_call_target="tpu_custom_call" | custom-call | flops 13958643712 | bytes 16777216 | tf_op jit(solution)/shard_map/pallas_call | solution.py:573
  138.9 2.2 %copy.13 = f32[192,1280]{1,0:T(8,128)} copy(f32[192,1280]{1,0:T(8,128)} %shard_map.100) | data formatting | bytes 1966080

commit v3 on v2

--- a/solution.py
+++ b/solution.py
@@ -128,11 +128,11 @@
     out,
     wq, em, gr, wm, mp, slope,
     x, part, part_in, sums, grads,
-    x_send, x_in, r_send, r_in, gains, rows_at,
-    h_send, h, q, q_in, u, w, f,
+    em_rows, gr_rows, ng, stat, rows_at,
+    h, q, q_in, u, w, f,
     local_sem, x_s, x_r, part_s, part_r, sums_s, grads_r,
-    em_s, em_r, gr_s, gr_r, gain_s, gain_r, at_s, at_r,
-    hs_s, h_s, h_r, q_s, q_r, u_s, w_r, w_s, f_r,
+    ng_s, ng_r, stat_s, stat_r, at_s, at_r,
+    h_s, h_r, q_s, q_r, u_s, w_r, w_s, f_r,
 ):
     s = lax.axis_index("dp")
     t = lax.axis_index("tensor")
@@ -143,7 +143,8 @@
     sibling = (sib, t)
     tokens = gq.shape[0]
     image_count = pos.shape[1]
-    rows = image_count // PARTS
+    half = image_count // 2
+    rows = half // PARTS
     block = wq.shape[0]
     width = block * groups
     hidden = wm.shape[0]
@@ -171,26 +172,19 @@
             hot, ref[...], (((0,), (0,)), ((), ())), preferred_element_type=F32
         ).astype(BF16)
 
-    x[pl.ds(s, 1)] = pick(gq)[None]
+    x[pl.ds(s, 1)] = pick(gq).reshape(1, 2, half, -1)
     pl.semaphore_wait(barrier, groups - 1 + PARTS - 1)
 
-    def to_right(b, d):
-        return remote(x.at[b], x.at[b], x_s.at[b, 0], x_r.at[b], (s + CORES, t))
-
-    def to_left(b, d):
-        return remote(x.at[b], x.at[b], x_s.at[b, 1], x_r.at[b], (s - CORES, t))
-
-    def to_sibling(b, d):
-        return remote(x.at[b], x.at[b], x_s.at[b, 2], x_r.at[b], sibling)
-
-    def h_right(b, d):
-        return remote(h.at[b, d], h.at[b, d], h_s.at[b, d, 0], h_r.at[b, d], (s + CORES, t))
-
-    def h_left(b, d):
-        return remote(h.at[b, d], h.at[b, d], h_s.at[b, d, 1], h_r.at[b, d], (s - CORES, t))
-
-    def h_sibling(b, d):
-        return remote(h.at[b, d], h.at[b, d], h_s.at[b, d, 2], h_r.at[b, d], sibling)
+    def kinds_of(ref, send, recv):
+        def make(side, device):
+            return lambda b, d: remote(
+                ref.at[b, d], ref.at[b, d], send.at[b, d, side], recv.at[b, d], device
+            )
+
+        return make(0, (s + CORES, t)), make(1, (s - CORES, t)), make(2, sibling)
+
+    x_kinds = kinds_of(x, x_s, x_r)
+    h_kinds = kinds_of(h, h_s, h_r)
 
     def spread(act, kinds, zz, d):
         b = zz * CORES + c
@@ -212,32 +206,18 @@
     def sent(copy):
         copy.wait_send()
 
-    x_kinds = (to_right, to_left, to_sibling)
-    h_kinds = (h_right, h_left, h_sibling)
-    spread(start, x_kinds, z, 0)
-
     def peer(k):
         return (t + k) % PARTS
 
-    gains[pl.ds(t, 1)] = jnp.broadcast_to(gain[...], (1, 8, gain.shape[1]))
-    loads[0].wait()
-    x_send[...] = pick(em).reshape(x_send.shape)
-    loads[1].wait()
-    r_send[...] = pick(gr).reshape(r_send.shape)
-
-    def row_copies(k):
-        p = peer(k)
-        return (
-            remote(x_send.at[p], x_in.at[t], em_s.at[k], em_r.at[t], (s, p)),
-            remote(r_send.at[p], r_in.at[t], gr_s.at[k], gr_r.at[t], (s, p)),
-            remote(gains.at[t], gains.at[t], gain_s.at[k], gain_r.at[t], (s, p)),
-        )
-
-    for k in range(1, PARTS):
-        for copy in row_copies(k):
-            copy.start()
-    x_in[pl.ds(t, 1)] = x_send[pl.ds(t, 1)]
-    r_in[pl.ds(t, 1)] = r_send[pl.ds(t, 1)]
+    def arrived(ref, sem):
+        remote(ref, ref, x_s.at[0, 0, 0], sem, sibling).wait_recv()
+
+    def pass_on(ref, recv, kinds, zz, d):
+        b = zz * CORES + c
+        arrived(ref.at[b, d], recv.at[b, d])
+        spread(start, kinds, zz, d)
+
+    spread(start, x_kinds, z, 0)
 
     lane = lax.broadcasted_iota(jnp.int32, (groups, image_count), 1)
     hot_dest = (dest[...] == lax.broadcasted_iota(jnp.int32, (groups, image_count), 0)) & (lane < count[0])
@@ -259,68 +239,140 @@
     for k in range(1, groups):
         at_copy(k).start()
 
-    def part_copy(zz, k):
+    def part_copy(d, zz, k):
         p = peer(k)
-        return remote(part.at[zz, p], part_in.at[zz, t], part_s.at[zz, k], part_r.at[zz, t], (s, p))
-
-    def sums_copy(zz, cc):
         return remote(
-            sums.at[zz, cc], grads.at[s], sums_s.at[zz, cc], grads_r.at[s], (zz * CORES + cc, t)
+            part.at[d, zz, p], part_in.at[d, zz, t], part_s.at[d, zz, k], part_r.at[d, zz, t], (s, p)
         )
 
-    def arrived(ref, sem):
-        remote(ref, ref, x_s.at[0, 0], sem, sibling).wait_recv()
-
-    def add_parts(zz):
-        total = part[zz, t].astype(F32)
+    def sums_copy(d, zz, cc):
+        return remote(
+            sums.at[d, zz, cc], grads.at[d, s], sums_s.at[d, zz, cc], grads_r.at[d, s],
+            (zz * CORES + cc, t),
+        )
+
+    def add_parts(g):
+        d = g // Z
+        zz = stage_order(z, g % Z)
+        total = part[d, zz, t].astype(F32)
         for k in range(1, PARTS):
             p = peer(k)
-            arrived(part_in.at[zz, p], part_r.at[zz, p])
-            total += part_in[zz, p].astype(F32)
-        sums[pl.ds(zz, 1)] = total.astype(BF16)[None]
+            arrived(part_in.at[d, zz, p], part_r.at[d, zz, p])
+            total += part_in[d, zz, p].astype(F32)
+        sums[pl.ds(d, 1), pl.ds(zz, 1)] = total.astype(BF16)[None, None]
         for cc in range(CORES):
             own = (zz == z) & (c == cc)
 
             @pl.when(jnp.logical_not(own))
             def _():
-                sums_copy(zz, cc).start()
+                sums_copy(d, zz, cc).start()
 
             @pl.when(own)
             def _():
-                grads[pl.ds(s, 1)] = sums[zz, cc][None]
+                grads[pl.ds(d, 1), pl.ds(s, 1)] = sums[d, zz, cc][None, None]
+
+    def grad_copy(d, k):
+        p = peer(k)
+        return remote(
+            grads.at[d, pl.ds(p * 2, 2)], ng.at[d, t], ng_s.at[d, k], ng_r.at[d, t], (s, p)
+        )
+
+    def norm_send(d):
+        for k in range(1, groups):
+            b = (s + k) % groups
+            arrived(grads.at[d, b], grads_r.at[d, b])
+        for k in range(1, PARTS):
+            grad_copy(d, k).start()
+        ng[d, pl.ds(t, 1)] = grads[d, pl.ds(t * 2, 2)][None]
+
+    def stat_copy(d, k):
+        return remote(stat.at[d, t], stat.at[d, t], stat_s.at[d, k], stat_r.at[d, t], (s, peer(k)))
+
+    def pieces(d, p):
+        for e in range(2):
+            lo = e * block
+            top = d * half + p * rows
+            value = em_rows[top:top + rows, lo:lo + block].astype(F32)
+            yield lo, top, value, gain[:, lo:lo + block] * ng[d, p, e].astype(F32)
+
+    def norm_stats(d):
+        for k in range(1, PARTS):
+            p = peer(k)
+            arrived(ng.at[d, p], ng_r.at[d, p])
+        side = lax.broadcasted_iota(jnp.int32, (rows, 128), 1)
+        for p in range(PARTS):
+            squares = jnp.zeros((rows, 1), F32)
+            inner = jnp.zeros((rows, 1), F32)
+            for lo, top, value, scaled in pieces(d, p):
+                squares += jnp.sum(value * value, axis=1, keepdims=True)
+                inner += jnp.sum(scaled * value, axis=1, keepdims=True)
+            both = jnp.where(side < 64, squares, inner)
+            stat[d, pl.ds(t, 1), p * rows:(p + 1) * rows] = both[None]
+        for k in range(1, PARTS):
+            stat_copy(d, k).start()
+
+    def norm_finish(d):
+        for k in range(1, PARTS):
+            p = peer(k)
+            arrived(stat.at[d, p], stat_r.at[d, p])
+        for p in range(PARTS):
+            total = jnp.zeros((rows, 128), F32)
+            for src in range(PARTS):
+                total += stat[d, src, p * rows:(p + 1) * rows]
+            inverse = lax.rsqrt(total[:, 0:1] / width + NORM_EPS)
+            back = inverse * inverse * inverse * total[:, 64:65] / width
+            for lo, top, value, scaled in pieces(d, p):
+                residual = gr_rows[top:top + rows, lo:lo + block].astype(F32)
+                result = residual + inverse * scaled - value * back
+                h[pl.ds(s, 1), d, p * rows:(p + 1) * rows, lo:lo + block] = result.astype(BF16)[None]
+        spread(start, h_kinds, z, d)
 
     loads[2].wait()
 
-    def pass_on(zz):
-        b = zz * CORES + c
-        arrived(x.at[b], x_r.at[b])
-        spread(start, x_kinds, zz, 0)
-
-    def first_step(step, carry):
+    def first_step(g, carry):
+        d, step = g // Z, g % Z
         zz = stage_order(z, step)
-
-        @pl.when((step == 1) | (step == 3) | ((step == 2) & jnp.logical_not(middle)))
-        def _():
-            pass_on(zz)
+        passes = (step == 1) | (step == 3) | ((step == 2) & jnp.logical_not(middle))
+        late = (g == 2 * Z - 1) & jnp.logical_not(middle)
+
+        @pl.when(passes & jnp.logical_not(late))
+        def _():
+            pass_on(x, x_r, x_kinds, zz, d)
 
         @pl.when((step == 1) & middle)
         def _():
-            pass_on(stage_order(z, 2))
+            pass_on(x, x_r, x_kinds, stage_order(z, 2), d)
+
+        @pl.when(((g == 3) & middle) | ((g == 1) & jnp.logical_not(middle)))
+        def _():
+            spread(start, x_kinds, z, 1)
+
+        @pl.when(g == 2 * Z - 1)
+        def _():
+            norm_stats(0)
+
+        @pl.when(late)
+        def _():
+            pass_on(x, x_r, x_kinds, zz, d)
 
         b = zz * CORES + 1 - c
-        arrived(x.at[b], x_r.at[b])
-        left = x[pl.ds(zz * CORES, CORES)].reshape(CORES * image_count, -1)
+        arrived(x.at[b, d], x_r.at[b, d])
+        left = x[pl.ds(zz * CORES, CORES), pl.ds(d, 1)].reshape(CORES * half, -1)
         tile = 256
         for n in range(0, block, tile):
             piece = transposed_product(left, wq[n:n + tile]).astype(BF16)
             piece = piece.reshape(CORES, PARTS, rows, tile)
             for p in range(PARTS):
-                part[pl.ds(zz, 1), p, :, :, n:n + tile] = piece[:, p][None]
-        for k in range(1, PARTS):
-            part_copy(zz, k).start()
-
-        @pl.when(step == 0)
-        def _():
+                part[pl.ds(d, 1), pl.ds(zz, 1), p, :, :, n:n + tile] = piece[:, p][None, None]
+        for k in range(1, PARTS):
+            part_copy(d, zz, k).start()
+
+        @pl.when(g == 0)
+        def _():
+            loads[0].wait()
+            em_rows[...] = pick(em)
+            loads[1].wait()
+            gr_rows[...] = pick(gr)
             loads[3].wait()
 
             def some_rows(i, carry):
@@ -330,58 +382,32 @@
 
             lax.fori_loop(0, mp.shape[0] // UNIT, some_rows, 0)
 
-        @pl.when(step > 0)
-        def _():
-            add_parts(stage_order(z, step - 1))
+        @pl.when(g == 2 * Z - 1)
+        def _():
+            norm_finish(0)
+
+        @pl.when(g > 0)
+        def _():
+            add_parts(g - 1)
+
+        @pl.when(g == 2 * Z - 2)
+        def _():
+            norm_send(0)
 
         return carry
 
-    lax.fori_loop(0, Z, first_step, 0)
-    for k in range(1, PARTS):
-        p = peer(k)
-        arrived(x_in.at[p], em_r.at[p])
-        arrived(r_in.at[p], gr_r.at[p])
-        arrived(gains.at[p], gain_r.at[p])
-    squares = jnp.zeros((rows, 1), F32)
-    for p in range(PARTS):
-        value = x_in[p].astype(F32)
-        squares += jnp.sum(value * value, axis=1, keepdims=True)
-    inverse = lax.rsqrt(squares / width + NORM_EPS)
-    add_parts(stage_order(z, Z - 1))
-
-    for k in range(1, groups):
-        b = (s + k) % groups
-        arrived(grads.at[b], grads_r.at[b])
-
-    def scaled_block(b):
-        lo = (b % 2) * block
-        return gains[b // 2, 0:1, lo:lo + block] * grads[b].astype(F32)
-
-    inner = jnp.zeros((rows, 1), F32)
-    for b in range(groups):
-        lo = (b % 2) * block
-        value = x_in[b // 2, :, lo:lo + block].astype(F32)
-        inner += jnp.sum(scaled_block(b) * value, axis=1, keepdims=True)
-    back = inverse * inverse * inverse * inner / width
-    for b in range(groups):
-        lo = (b % 2) * block
-        value = x_in[b // 2, :, lo:lo + block].astype(F32)
-        residual = r_in[b // 2, :, lo:lo + block].astype(F32)
-        result = residual + inverse * scaled_block(b) - value * back
-        h_send[b // 2, :, lo:lo + block] = result.astype(BF16)
-
-    def hand_copy(k):
-        p = peer(k)
-        return remote(h_send.at[p], h.at[s, t], hs_s.at[k], h_r.at[s, t], (s, p))
-
-    for k in range(1, PARTS):
-        hand_copy(k).start()
-    h[pl.ds(s, 1), pl.ds(t, 1)] = h_send[pl.ds(t, 1)][None]
-    for k in range(PARTS):
-        d = peer(k)
-        if k:
-            arrived(h.at[s, d], h_r.at[s, d])
-        spread(start, h_kinds, z, d)
+    lax.fori_loop(0, 2 * Z, first_step, 0)
+    add_parts(2 * Z - 1)
+
+    pass_on(h, h_r, h_kinds, stage_order(z, 1), 0)
+
+    @pl.when(middle)
+    def _():
+        pass_on(h, h_r, h_kinds, stage_order(z, 2), 0)
+
+    norm_send(1)
+    norm_stats(1)
+    norm_finish(1)
 
     for k in range(1, groups):
         b = (s + k) % groups
@@ -413,26 +439,24 @@
                 u_copy(zz, (s + k) % groups).start()
             w[pl.ds(s, 1), pl.ds(zz, 1)] = u[zz, s][None, None]
 
-    def h_pass(zz, k):
-        b = zz * CORES + c
-        d = peer(k)
-        arrived(h.at[b, d], h_r.at[b, d])
-        spread(start, h_kinds, zz, d)
-
     def second_step(step, carry):
         zz = stage_order(z, step)
-        for k in range(PARTS):
-            @pl.when((step == 1) | (step == 3) | ((step == 2) & jnp.logical_not(middle)))
-            def _():
-                h_pass(zz, k)
-
-            @pl.when((step == 1) & middle)
-            def _():
-                h_pass(stage_order(z, 2), k)
+        ends = jnp.logical_not(middle)
+
+        @pl.when((step == 1) | ((step > 1) & ends))
+        def _():
+            @pl.when(step > 1)
+            def _():
+                pass_on(h, h_r, h_kinds, zz, 0)
+
+            pass_on(h, h_r, h_kinds, zz, 1)
+
+        @pl.when((step == 1) & middle)
+        def _():
+            pass_on(h, h_r, h_kinds, stage_order(z, 2), 1)
 
         b = zz * CORES + 1 - c
-        for k in range(PARTS):
-            d = peer(k)
+        for d in range(2):
             arrived(h.at[b, d], h_r.at[b, d])
         left = h[pl.ds(zz * CORES, CORES)].reshape(CORES * image_count, -1)
         spots = jnp.concatenate([rows_at[zz * CORES, 0:1], rows_at[zz * CORES + 1, 0:1]], axis=1)
@@ -451,6 +475,11 @@
             def _():
                 q_copy(zz, k).start()
 
+        @pl.when((step == 2) & middle)
+        def _():
+            for d in range(2):
+                pass_on(h, h_r, h_kinds, stage_order(z, 3), d)
+
         @pl.when(step > 0)
         def _():
             add_units(stage_order(z, step - 1))
@@ -502,28 +531,28 @@
 
     lax.fori_loop(0, Z * UNITS, finish, 0)
 
-    for k in range(1, PARTS):
-        for copy in row_copies(k):
-            sent(copy)
-        sent(hand_copy(k))
     for k in range(1, groups):
         sent(at_copy(k))
+    for d in range(2):
+        for k in range(1, PARTS):
+            sent(grad_copy(d, k))
+            sent(stat_copy(d, k))
 
     def all_sent(zz, carry):
-        spread(sent, x_kinds, zz, 0)
-        for d in range(PARTS):
+        for d in range(2):
+            spread(sent, x_kinds, zz, d)
             spread(sent, h_kinds, zz, d)
-        for k in range(1, PARTS):
-            sent(part_copy(zz, k))
-
+            for k in range(1, PARTS):
+                sent(part_copy(d, zz, k))
+            for cc in range(CORES):
+                @pl.when((zz != z) | (c != cc))
+                def _():
+                    sent(sums_copy(d, zz, cc))
+
+        for k in range(1, PARTS):
             @pl.when(unit_of(peer(k), zz) < UNITS)
             def _():
                 sent(q_copy(zz, k))
-
-        for cc in range(CORES):
-            @pl.when((zz != z) | (c != cc))
-            def _():
-                sent(sums_copy(zz, cc))
 
         @pl.when(unit_of(t, zz) < UNITS)
         def _():
@@ -543,7 +572,8 @@
     groups = Z * CORES
     capacity = merge_pre.shape[0] // groups
     image_count = img_pos.shape[1]
-    rows = image_count // PARTS
+    half = image_count // 2
+    rows = half // PARTS
     block, columns = query_weight.shape
     hidden = merge_weight.shape[0]
     vmem = pltpu.VMEM
@@ -553,21 +583,20 @@
     scratch = [
         vmem(query_weight.shape, BF16), vmem(embeds.shape, BF16), vmem(grad_resid.shape, BF16),
         vmem(merge_weight.shape, BF16), vmem(merge_pre.shape, BF16), vmem(merge_pre.shape, F32),
-        vmem((groups, image_count, columns), BF16),
-        vmem((Z, PARTS, CORES, rows, block), BF16), vmem((Z, PARTS, CORES, rows, block), BF16),
-        vmem((Z, CORES, rows, block), BF16), vmem((groups, rows, block), BF16),
-        vmem((PARTS, rows, columns), BF16), vmem((PARTS, rows, columns), BF16),
-        vmem((PARTS, rows, columns), BF16), vmem((PARTS, rows, columns), BF16),
-        vmem((PARTS, 8, columns), F32), vmem((groups, 8, image_count), jnp.int32),
-        vmem((PARTS, rows, columns), BF16), vmem((groups, PARTS, rows, columns), BF16),
+        vmem((groups, 2, half, columns), BF16),
+        vmem((2, Z, PARTS, CORES, rows, block), BF16), vmem((2, Z, PARTS, CORES, rows, block), BF16),
+        vmem((2, Z, CORES, rows, block), BF16), vmem((2, groups, rows, block), BF16),
+        vmem((image_count, columns), BF16), vmem((image_count, columns), BF16),
+        vmem((2, PARTS, 2, rows, block), BF16), vmem((2, PARTS, half, 128), F32),
+        vmem((groups, 8, image_count), jnp.int32),
+        vmem((groups, 2, half, columns), BF16),
         vmem((Z, UNITS, groups, UNIT, hidden), BF16), vmem((Z, PARTS, groups, UNIT, hidden), BF16),
         vmem((Z, groups, UNIT, hidden), BF16), vmem((groups, Z, UNIT, hidden), BF16),
         vmem((Z * UNITS, 2, UNIT, hidden), BF16),
-        dma((5,)), dma((groups, 3)), dma((groups,)), dma((Z, PARTS)), dma((Z, PARTS)),
-        dma((Z, CORES)), dma((groups,)),
-        dma((PARTS,)), dma((PARTS,)), dma((PARTS,)), dma((PARTS,)), dma((PARTS,)), dma((PARTS,)),
-        dma((groups,)), dma((groups,)),
-        dma((PARTS,)), dma((groups, PARTS, 3)), dma((groups, PARTS)), dma((Z, PARTS)), dma((Z, PARTS)),
+        dma((5,)), dma((groups, 2, 3)), dma((groups, 2)), dma((2, Z, PARTS)), dma((2, Z, PARTS)),
+        dma((2, Z, CORES)), dma((2, groups)),
+        dma((2, PARTS)), dma((2, PARTS)), dma((2, PARTS)), dma((2, PARTS)), dma((groups,)), dma((groups,)),
+        dma((groups, 2, 3)), dma((groups, 2)), dma((Z, PARTS)), dma((Z, PARTS)),
         dma((Z, groups)), dma((groups, Z)), dma((groups, Z)), dma((Z * UNITS, 2)),
     ]
     return pl.pallas_call(

time: 141 us -> 136 us (0.965)
  Pallas kernels: 138 us -> 133 us
    pallas_call x1, Pallas kernels: 138 us -> 133 us  [fused(): pl.pallas_call(functools.partial(fused_kernel, capacity), out_shape=jax.S...]
where the time goes in v3:
time: 136 us; the launch traced here: 135 us
  Pallas kernels  133 us (98%)
  local copies, waits for them, and re-layouts  2.21 us (2%)
    pallas_call x1, Pallas kernels, fused(): pl.pallas_call(functools.partial(fused_kernel, capacity), out_shape=jax.S...  133 us

profile of v3, /device:TPU:0, one launch (start us, length us, event | category | flops | bytes accessed | tf_op | source)
XLA Modules:
  0.0 135.4 jit_solution(10958874919432617556)
XLA Ops:
  0.7 132.5 %shard_map.100 = f32[192,1280]{1,0:T(8,128)} custom-call(bf16[256,2048]{1,0:T(8,128)(2,1)} %gq.1, s32[1,128]{1,0:T(1,128)} %pos.1, s32[1]{0:T(128)S(6)} %copy.12.count, s32[1,128]{1,0:T(1,128)} %dest.1, f32[1,2048]{1,0:T(1,128)} %bitcast.1, bf16[1024,2048]{1,0:T(8,128)(2,1)} %wq_hbm.1, bf16[256,2048]{1,0:T(8,128)(2,1)} %em_hbm.1, bf16[256,2048]{1,0:T(8,128)(2,1)} %gr_hbm.1, ...), custom_call_target="tpu_custom_call" | custom-call | flops 13958643712 | bytes 16777216 | tf_op jit(solution)/shard_map/pallas_call | solution.py:602
  133.2 2.2 %copy.13 = f32[192,1280]{1,0:T(8,128)} copy(f32[192,1280]{1,0:T(8,128)} %shard_map.100) | data formatting | bytes 1966080

commit v4 on v3

--- a/solution.py
+++ b/solution.py
@@ -104,7 +104,7 @@
 CORES = 2
 PARTS = 4
 UNIT = 16
-UNITS = 3
+TILE = 128
 MESH = pl.DeviceIdType.MESH
 BF16 = jnp.bfloat16
 F32 = jnp.float32
@@ -148,6 +148,8 @@
     block = wq.shape[0]
     width = block * groups
     hidden = wm.shape[0]
+    tiles = hidden // TILE
+    pair_rows = CORES * capacity
     middle = (z == 1) | (z == 2)
 
     loads = [
@@ -229,8 +231,7 @@
     earlier = jnp.dot(hot_dest, before, preferred_element_type=F32)
     slot = jnp.sum(earlier * hot_dest, axis=0, keepdims=True).astype(jnp.int32)
     spot = c * capacity + slot
-    at = lax.shift_right_logical(spot, 4) * (groups * UNIT) + dest[...] * UNIT + (spot & (UNIT - 1))
-    at = jnp.where(lane[:1] < count[0], at, -1)
+    at = jnp.where(lane[:1] < count[0], dest[...] * pair_rows + spot, -1)
     rows_at[pl.ds(s, 1)] = jnp.broadcast_to(at, (1, 8, image_count))
 
     def at_copy(k):
@@ -414,122 +415,132 @@
         arrived(rows_at.at[b], at_r.at[b])
     loads[4].wait()
 
-    def unit_of(p, zz):
-        return (p + zz) % PARTS
-
-    def q_copy(zz, k):
-        p = peer(k)
+    def first_tile(zz):
+        return (t + PARTS - zz) % PARTS
+
+    def held(zz, e):
+        return (first_tile(zz) == 0) | (e == 0)
+
+    def tile_of(zz, e):
+        return first_tile(zz) if e == 0 else PARTS
+
+    def q_copy(zz, d, j):
+        e = j // PARTS
         return remote(
-            q.at[zz, unit_of(p, zz)], q_in.at[zz, t], q_s.at[zz, k], q_r.at[zz, t], (s, p)
+            q.at[zz, d, j], q_in.at[zz, d, e, t], q_s.at[zz, d, j], q_r.at[zz, d, e, t],
+            (s, (j + zz) % PARTS),
         )
 
-    def u_copy(zz, r):
-        return remote(u.at[zz, r], w.at[s, zz], u_s.at[zz, r], w_r.at[s, zz], (r, t))
-
-    def add_units(zz):
-        @pl.when(unit_of(t, zz) < UNITS)
-        def _():
-            total = q[zz, unit_of(t, zz)].astype(F32)
-            for k in range(1, PARTS):
-                p = peer(k)
-                arrived(q_in.at[zz, p], q_r.at[zz, p])
-                total += q_in[zz, p].astype(F32)
-            u[pl.ds(zz, 1)] = total.astype(BF16)[None]
-            for k in range(1, groups):
-                u_copy(zz, (s + k) % groups).start()
-            w[pl.ds(s, 1), pl.ds(zz, 1)] = u[zz, s][None, None]
-
-    def second_step(step, carry):
+    def u_copy(zz, e, r):
+        return remote(u.at[zz, e, r], w.at[s, zz, e], u_s.at[zz, e, r], w_r.at[s, zz, e], (r, t))
+
+    def add_tiles(zz):
+        places = []
+        for d in range(2):
+            lo = d * half
+            spots = jnp.concatenate(
+                [rows_at[zz * CORES + cc, 0:1, lo:lo + half] for cc in range(CORES)], axis=1
+            )
+            hot_rows = lax.broadcasted_iota(jnp.int32, (groups * pair_rows, CORES * half), 0) == spots
+            places.append(hot_rows.astype(F32).astype(BF16))
+        for e in range(2):
+            @pl.when(held(zz, e))
+            def _():
+                placed = jnp.zeros((groups * pair_rows, TILE), F32)
+                for d in range(2):
+                    total = q[zz, d, tile_of(zz, e)].astype(F32)
+                    for k in range(1, PARTS):
+                        p = peer(k)
+                        arrived(q_in.at[zz, d, e, p], q_r.at[zz, d, e, p])
+                        total += q_in[zz, d, e, p].astype(F32)
+                    placed += jnp.dot(places[d], total.astype(BF16), preferred_element_type=F32)
+                placed = placed.astype(BF16).reshape(1, 1, groups, pair_rows, TILE)
+                u[pl.ds(zz, 1), e:e + 1] = placed
+                for k in range(1, groups):
+                    u_copy(zz, e, (s + k) % groups).start()
+                w[pl.ds(s, 1), pl.ds(zz, 1), e] = u[zz, e, s][None, None]
+
+    def second_step(i, carry):
+        step, d = i // 2, i % 2
         zz = stage_order(z, step)
         ends = jnp.logical_not(middle)
 
-        @pl.when((step == 1) | ((step > 1) & ends))
-        def _():
-            @pl.when(step > 1)
+        @pl.when((i == 3) | ((i > 3) & ends))
+        def _():
+            pass_on(h, h_r, h_kinds, zz, d)
+
+        @pl.when((i == 3) & middle)
+        def _():
+            pass_on(h, h_r, h_kinds, stage_order(z, 2), 1)
+
+        b = zz * CORES + 1 - c
+        arrived(h.at[b, d], h_r.at[b, d])
+        left = h[pl.ds(zz * CORES, CORES), pl.ds(d, 1)].reshape(CORES * half, -1)
+        for j in range(0, tiles, 2):
+            hi = min(j + 2, tiles)
+            piece = transposed_product(left, wm[j * TILE:hi * TILE]).astype(BF16)
+            for jj in range(j, hi):
+                q[pl.ds(zz, 1), pl.ds(d, 1), jj] = piece[:, (jj - j) * TILE:(jj - j + 1) * TILE][None, None]
+        for j in range(tiles):
+            @pl.when((j + zz) % PARTS != t)
             def _():
-                pass_on(h, h_r, h_kinds, zz, 0)
-
-            pass_on(h, h_r, h_kinds, zz, 1)
-
-        @pl.when((step == 1) & middle)
-        def _():
-            pass_on(h, h_r, h_kinds, stage_order(z, 2), 1)
-
-        b = zz * CORES + 1 - c
-        for d in range(2):
-            arrived(h.at[b, d], h_r.at[b, d])
-        left = h[pl.ds(zz * CORES, CORES)].reshape(CORES * image_count, -1)
-        spots = jnp.concatenate([rows_at[zz * CORES, 0:1], rows_at[zz * CORES + 1, 0:1]], axis=1)
-        placed_rows = UNITS * groups * UNIT
-        place = lax.broadcasted_iota(jnp.int32, (placed_rows, CORES * image_count), 0) == spots
-        place = place.astype(F32).astype(BF16)
-        lo = 0
-        while lo < hidden:
-            hi = min(lo + 256, hidden)
-            piece = transposed_product(left, wm[lo:hi]).astype(BF16)
-            piece = jnp.dot(place, piece, preferred_element_type=F32).astype(BF16)
-            q[pl.ds(zz, 1), :, :, :, lo:hi] = piece.reshape(1, UNITS, groups, UNIT, hi - lo)
-            lo = hi
-        for k in range(1, PARTS):
-            @pl.when(unit_of(peer(k), zz) < UNITS)
-            def _():
-                q_copy(zz, k).start()
-
-        @pl.when((step == 2) & middle)
-        def _():
-            for d in range(2):
-                pass_on(h, h_r, h_kinds, stage_order(z, 3), d)
-
-        @pl.when(step > 0)
-        def _():
-            add_units(stage_order(z, step - 1))
+                q_copy(zz, d, j).start()
+
+        @pl.when(((i == 3) | (i == 5)) & middle)
+        def _():
+            pass_on(h, h_r, h_kinds, stage_order(z, 3), i // 5)
+
+        @pl.when((i > 1) & (d == 0))
+        def _():
+            add_tiles(stage_order(z, step - 1))
 
         return carry
 
-    lax.fori_loop(0, Z, second_step, 0)
-    add_units(stage_order(z, Z - 1))
-
-    def f_copy(b, zz):
-        unit = zz * UNITS + unit_of(t, zz)
-        return remote(w.at[b, zz], f.at[unit, b % 2], w_s.at[b, zz], f_r.at[unit, b % 2], (s, b // 2))
+    lax.fori_loop(0, 2 * Z, second_step, 0)
+    add_tiles(stage_order(z, Z - 1))
+
+    def f_copy(b, zz, e):
+        j = tile_of(zz, e)
+        return remote(
+            w.at[b, zz, e], f.at[zz, b % 2, j], w_s.at[b, zz, e], f_r.at[zz, b % 2, j], (s, b // 2)
+        )
 
     def hand_out(i, carry):
         step, k = i // groups, i % groups
         b = (s + k) % groups
         zz = stage_order(b // CORES, step)
-
-        @pl.when(unit_of(t, zz) < UNITS)
-        def _():
-            @pl.when(b != s)
+        for e in range(2):
+            @pl.when(held(zz, e))
             def _():
-                arrived(w.at[b, zz], w_r.at[b, zz])
-
-            @pl.when(b // 2 != t)
-            def _():
-                f_copy(b, zz).start()
-
-            @pl.when(b // 2 == t)
-            def _():
-                unit = zz * UNITS + unit_of(t, zz)
-                f[pl.ds(unit, 1), pl.ds(b % 2, 1)] = w[b, zz][None, None]
+                @pl.when(b != s)
+                def _():
+                    arrived(w.at[b, zz, e], w_r.at[b, zz, e])
+
+                @pl.when(b // 2 != t)
+                def _():
+                    f_copy(b, zz, e).start()
+
+                @pl.when(b // 2 == t)
+                def _():
+                    f[pl.ds(zz, 1), pl.ds(b % 2, 1), pl.ds(tile_of(zz, e), 1)] = w[b, zz, e][None, None, None]
 
         return carry
 
     lax.fori_loop(0, Z * groups, hand_out, 0)
 
-    def finish(unit, carry):
-        zz, k = unit // UNITS, unit % UNITS
-        span = pl.ds(pl.multiple_of(unit * UNIT, UNIT), UNIT)
-        for half in range(2):
-            @pl.when((k + PARTS - zz) % PARTS != t)
-            def _():
-                arrived(f.at[unit, half], f_r.at[unit, half])
-
-            columns = slice(half * hidden, (half + 1) * hidden)
-            out[span, columns] = f[unit, half].astype(F32) * slope[span, columns]
+    def finish(zz, carry):
+        span = pl.ds(pl.multiple_of(zz * pair_rows, pair_rows), pair_rows)
+        for side in range(2):
+            for j in range(tiles):
+                @pl.when((j + zz) % PARTS != t)
+                def _():
+                    arrived(f.at[zz, side, j], f_r.at[zz, side, j])
+
+                lo = side * hidden + j * TILE
+                out[span, lo:lo + TILE] = f[zz, side, j].astype(F32) * slope[span, lo:lo + TILE]
         return carry
 
-    lax.fori_loop(0, Z * UNITS, finish, 0)
+    lax.fori_loop(0, Z, finish, 0)
 
     for k in range(1, groups):
         sent(at_copy(k))
@@ -549,19 +560,21 @@
                 def _():
                     sent(sums_copy(d, zz, cc))
 
-        for k in range(1, PARTS):
-            @pl.when(unit_of(peer(k), zz) < UNITS)
+        for j in range(tiles):
+            @pl.when((j + zz) % PARTS != t)
             def _():
-                sent(q_copy(zz, k))
-
-        @pl.when(unit_of(t, zz) < UNITS)
-        def _():
-            for k in range(1, groups):
-                sent(u_copy(zz, (s + k) % groups))
-            for b in range(groups):
-                @pl.when(b // 2 != t)
-                def _():
-                    sent(f_copy(b, zz))
+                for d in range(2):
+                    sent(q_copy(zz, d, j))
+
+        for e in range(2):
+            @pl.when(held(zz, e))
+            def _():
+                for k in range(1, groups):
+                    sent(u_copy(zz, e, (s + k) % groups))
+                for b in range(groups):
+                    @pl.when(b // 2 != t)
+                    def _():
+                        sent(f_copy(b, zz, e))
 
         return carry
 
@@ -575,7 +588,8 @@
     half = image_count // 2
     rows = half // PARTS
     block, columns = query_weight.shape
-    hidden = merge_weight.shape[0]
+    tiles = merge_weight.shape[0] // TILE
+    pair_rows = CORES * capacity
     vmem = pltpu.VMEM
     dma = pltpu.SemaphoreType.DMA
     in_vmem = pl.BlockSpec(memory_space=pltpu.VMEM)
@@ -590,14 +604,14 @@
         vmem((2, PARTS, 2, rows, block), BF16), vmem((2, PARTS, half, 128), F32),
         vmem((groups, 8, image_count), jnp.int32),
         vmem((groups, 2, half, columns), BF16),
-        vmem((Z, UNITS, groups, UNIT, hidden), BF16), vmem((Z, PARTS, groups, UNIT, hidden), BF16),
-        vmem((Z, groups, UNIT, hidden), BF16), vmem((groups, Z, UNIT, hidden), BF16),
-        vmem((Z * UNITS, 2, UNIT, hidden), BF16),
+        vmem((Z, 2, tiles, CORES * half, TILE), BF16), vmem((Z, 2, 2, PARTS, CORES * half, TILE), BF16),
+        vmem((Z, 2, groups, pair_rows, TILE), BF16), vmem((groups, Z, 2, pair_rows, TILE), BF16),
+        vmem((Z, 2, tiles, pair_rows, TILE), BF16),
         dma((5,)), dma((groups, 2, 3)), dma((groups, 2)), dma((2, Z, PARTS)), dma((2, Z, PARTS)),
         dma((2, Z, CORES)), dma((2, groups)),
         dma((2, PARTS)), dma((2, PARTS)), dma((2, PARTS)), dma((2, PARTS)), dma((groups,)), dma((groups,)),
-        dma((groups, 2, 3)), dma((groups, 2)), dma((Z, PARTS)), dma((Z, PARTS)),
-        dma((Z, groups)), dma((groups, Z)), dma((groups, Z)), dma((Z * UNITS, 2)),
+        dma((groups, 2, 3)), dma((groups, 2)), dma((Z, 2, tiles)), dma((Z, 2, 2, PARTS)),
+        dma((Z, 2, groups)), dma((groups, Z, 2)), dma((groups, Z, 2)), dma((Z, 2, tiles)),
     ]
     return pl.pallas_call(
         functools.partial(fused_kernel, capacity),
@@ -612,7 +626,7 @@
             collective_id=0, has_side_effects=True, vmem_limit_bytes=56 * 1024 * 1024
         ),
         cost_estimate=pl.CostEstimate(
-            flops=4 * groups * image_count * columns * (block + hidden),
+            flops=4 * groups * image_count * columns * (block + merge_weight.shape[0]),
             bytes_accessed=16 * 1024 * 1024,
             transcendentals=merge_pre.size,
         ),

time: 136 us -> 134 us (0.985)
  Pallas kernels: 133 us -> 131 us
where the time goes in v4:
time: 134 us
  Pallas kernels  131 us (98%)
  local copies, waits for them, and re-layouts  2.21 us (2%)
    pallas_call x1, Pallas kernels, fused(): pl.pallas_call(functools.partial(fused_kernel, capacity), out_shape=jax.S...  131 us

profile of v4, /device:TPU:0, one launch (start us, length us, event | category | flops | bytes accessed | tf_op | source)
XLA Modules:
  0.0 134.1 jit_solution(16843729559855591652)
XLA Ops:
  0.7 131.2 %shard_map.100 = f32[192,1280]{1,0:T(8,128)} custom-call(bf16[256,2048]{1,0:T(8,128)(2,1)} %gq.1, s32[1,128]{1,0:T(1,128)} %pos.1, s32[1]{0:T(128)S(6)} %copy.12.count, s32[1,128]{1,0:T(1,128)} %dest.1, f32[1,2048]{1,0:T(1,128)} %bitcast.1, bf16[1024,2048]{1,0:T(8,128)(2,1)} %wq_hbm.1, bf16[256,2048]{1,0:T(8,128)(2,1)} %em_hbm.1, bf16[256,2048]{1,0:T(8,128)(2,1)} %gr_hbm.1, ...), custom_call_target="tpu_custom_call" | custom-call | flops 13958643712 | bytes 16777216 | tf_op jit(solution)/shard_map/pallas_call | solution.py:616
  131.9 2.2 %copy.13 = f32[192,1280]{1,0:T(8,128)} copy(f32[192,1280]{1,0:T(8,128)} %shard_map.100) | data formatting | bytes 1966080

commit v5 on v4

--- a/solution.py
+++ b/solution.py
@@ -126,7 +126,7 @@
     capacity,
     gq, pos, count, dest, gain, wq_hbm, em_hbm, gr_hbm, wm_hbm, mp_hbm,
     out,
-    wq, em, gr, wm, mp, slope,
+    wq, em, gr, wm, mp, slope, wq_t, wm_t,
     x, part, part_in, sums, grads,
     em_rows, gr_rows, ng, stat, rows_at,
     h, q, q_in, u, w, f,
@@ -155,7 +155,7 @@
     loads = [
         pltpu.make_async_copy(src, dst, local_sem.at[i])
         for i, (src, dst) in enumerate(
-            ((em_hbm, em), (gr_hbm, gr), (wq_hbm, wq), (mp_hbm, mp), (wm_hbm, wm))
+            ((wq_hbm, wq), (em_hbm, em), (gr_hbm, gr), (wm_hbm, wm), (mp_hbm, mp))
         )
     ]
     for load in loads:
@@ -328,25 +328,33 @@
                 h[pl.ds(s, 1), d, p * rows:(p + 1) * rows, lo:lo + block] = result.astype(BF16)[None]
         spread(start, h_kinds, z, d)
 
-    loads[2].wait()
+    def turn(src, dst):
+        for lo in range(0, src.shape[0], TILE):
+            dst[:, lo:lo + TILE] = src[lo:lo + TILE].T
+
+    loads[0].wait()
+    turn(wq, wq_t)
+    pass_on(x, x_r, x_kinds, stage_order(z, 1), 0)
+
+    @pl.when(middle)
+    def _():
+        pass_on(x, x_r, x_kinds, stage_order(z, 2), 0)
+
+    spread(start, x_kinds, z, 1)
 
     def first_step(g, carry):
         d, step = g // Z, g % Z
         zz = stage_order(z, step)
-        passes = (step == 1) | (step == 3) | ((step == 2) & jnp.logical_not(middle))
+        passes = (g == Z + 1) | (step == 3) | ((step == 2) & jnp.logical_not(middle))
         late = (g == 2 * Z - 1) & jnp.logical_not(middle)
 
         @pl.when(passes & jnp.logical_not(late))
         def _():
             pass_on(x, x_r, x_kinds, zz, d)
 
-        @pl.when((step == 1) & middle)
+        @pl.when((g == Z + 1) & middle)
         def _():
             pass_on(x, x_r, x_kinds, stage_order(z, 2), d)
-
-        @pl.when(((g == 3) & middle) | ((g == 1) & jnp.logical_not(middle)))
-        def _():
-            spread(start, x_kinds, z, 1)
 
         @pl.when(g == 2 * Z - 1)
         def _():
@@ -361,20 +369,28 @@
         left = x[pl.ds(zz * CORES, CORES), pl.ds(d, 1)].reshape(CORES * half, -1)
         tile = 256
         for n in range(0, block, tile):
-            piece = transposed_product(left, wq[n:n + tile]).astype(BF16)
+            piece = jnp.dot(left, wq_t[:, n:n + tile], preferred_element_type=F32).astype(BF16)
             piece = piece.reshape(CORES, PARTS, rows, tile)
             for p in range(PARTS):
                 part[pl.ds(d, 1), pl.ds(zz, 1), p, :, :, n:n + tile] = piece[:, p][None, None]
         for k in range(1, PARTS):
             part_copy(d, zz, k).start()
 
-        @pl.when(g == 0)
-        def _():
-            loads[0].wait()
+        @pl.when(g == 1)
+        def _():
+            loads[1].wait()
             em_rows[...] = pick(em)
-            loads[1].wait()
+            loads[2].wait()
             gr_rows[...] = pick(gr)
+
+        @pl.when(g == 2)
+        def _():
             loads[3].wait()
+            turn(wm, wm_t)
+
+        @pl.when(g == 4)
+        def _():
+            loads[4].wait()
 
             def some_rows(i, carry):
                 span = pl.ds(pl.multiple_of(i * UNIT, UNIT), UNIT)
@@ -413,7 +429,6 @@
     for k in range(1, groups):
         b = (s + k) % groups
         arrived(rows_at.at[b], at_r.at[b])
-    loads[4].wait()
 
     def first_tile(zz):
         return (t + PARTS - zz) % PARTS
@@ -478,7 +493,7 @@
         left = h[pl.ds(zz * CORES, CORES), pl.ds(d, 1)].reshape(CORES * half, -1)
         for j in range(0, tiles, 2):
             hi = min(j + 2, tiles)
-            piece = transposed_product(left, wm[j * TILE:hi * TILE]).astype(BF16)
+            piece = jnp.dot(left, wm_t[:, j * TILE:hi * TILE], preferred_element_type=F32).astype(BF16)
             for jj in range(j, hi):
                 q[pl.ds(zz, 1), pl.ds(d, 1), jj] = piece[:, (jj - j) * TILE:(jj - j + 1) * TILE][None, None]
         for j in range(tiles):
@@ -597,6 +612,7 @@
     scratch = [
         vmem(query_weight.shape, BF16), vmem(embeds.shape, BF16), vmem(grad_resid.shape, BF16),
         vmem(merge_weight.shape, BF16), vmem(merge_pre.shape, BF16), vmem(merge_pre.shape, F32),
+        vmem(query_weight.shape[::-1], BF16), vmem(merge_weight.shape[::-1], BF16),
         vmem((groups, 2, half, columns), BF16),
         vmem((2, Z, PARTS, CORES, rows, block), BF16), vmem((2, Z, PARTS, CORES, rows, block), BF16),
         vmem((2, Z, CORES, rows, block), BF16), vmem((2, groups, rows, block), BF16),

time: 134 us -> 134 us (level)
  no operation moved by 1% of the time
where the time goes in v5:
time: 134 us
  Pallas kernels  131 us (98%)
  local copies, waits for them, and re-layouts  2.21 us (2%)
    pallas_call x1, Pallas kernels, fused(): pl.pallas_call(functools.partial(fused_kernel, capacity), out_shape=jax.S...  131 us

profile of v5, /device:TPU:0, one launch (start us, length us, event | category | flops | bytes accessed | tf_op | source)
XLA Modules:
  0.0 133.8 jit_solution(7786344923797505272)
XLA Ops:
  0.7 130.9 %shard_map.100 = f32[192,1280]{1,0:T(8,128)} custom-call(bf16[256,2048]{1,0:T(8,128)(2,1)} %gq.1, s32[1,128]{1,0:T(1,128)} %pos.1, s32[1]{0:T(128)S(6)} %copy.12.count, s32[1,128]{1,0:T(1,128)} %dest.1, f32[1,2048]{1,0:T(1,128)} %bitcast.1, bf16[1024,2048]{1,0:T(8,128)(2,1)} %wq_hbm.1, bf16[256,2048]{1,0:T(8,128)(2,1)} %em_hbm.1, bf16[256,2048]{1,0:T(8,128)(2,1)} %gr_hbm.1, ...), custom_call_target="tpu_custom_call" | custom-call | flops 13958643712 | bytes 16777216 | tf_op jit(solution)/shard_map/pallas_call | solution.py:632
  131.5 2.2 %copy.13 = f32[192,1280]{1,0:T(8,128)} copy(f32[192,1280]{1,0:T(8,128)} %shard_map.100) | data formatting | bytes 1966080

commit v6 on v5

--- a/solution.py
+++ b/solution.py
@@ -112,7 +112,7 @@
 
 def stage_order(z, step):
     near = jnp.where(z >= 2, Z - 1 - z, z)
-    at = jnp.where((near == 1) & (step < 2), 1 - step, step)
+    at = jnp.where((near == 1) & (step < 3), (step + 1) % 3, step)
     return jnp.where(z >= 2, Z - 1 - at, at)
 
 
@@ -417,11 +417,6 @@
     add_parts(2 * Z - 1)
 
     pass_on(h, h_r, h_kinds, stage_order(z, 1), 0)
-
-    @pl.when(middle)
-    def _():
-        pass_on(h, h_r, h_kinds, stage_order(z, 2), 0)
-
     norm_send(1)
     norm_stats(1)
     norm_finish(1)
@@ -480,13 +475,9 @@
         zz = stage_order(z, step)
         ends = jnp.logical_not(middle)
 
-        @pl.when((i == 3) | ((i > 3) & ends))
+        @pl.when((i >= 3) & (ends | (i < 6)))
         def _():
             pass_on(h, h_r, h_kinds, zz, d)
-
-        @pl.when((i == 3) & middle)
-        def _():
-            pass_on(h, h_r, h_kinds, stage_order(z, 2), 1)
 
         b = zz * CORES + 1 - c
         arrived(h.at[b, d], h_r.at[b, d])
@@ -501,9 +492,9 @@
             def _():
                 q_copy(zz, d, j).start()
 
-        @pl.when(((i == 3) | (i == 5)) & middle)
-        def _():
-            pass_on(h, h_r, h_kinds, stage_order(z, 3), i // 5)
+        @pl.when(((i == 4) | (i == 5)) & middle)
+        def _():
+            pass_on(h, h_r, h_kinds, stage_order(z, 3), d)
 
         @pl.when((i > 1) & (d == 0))
         def _():

time: 134 us -> 137 us (1.022)
  Pallas kernels: 131 us -> 134 us
    pallas_call x1, Pallas kernels: 131 us -> 134 us  [fused(): pl.pallas_call(functools.partial(fused_kernel, capacity), out_shape=jax.S...]
where the time goes in v6:
time: 137 us
  Pallas kernels  134 us (98%)
  local copies, waits for them, and re-layouts  2.21 us (2%)
    pallas_call x1, Pallas kernels, fused(): pl.pallas_call(functools.partial(fused_kernel, capacity), out_shape=jax.S...  134 us

profile of v6, /device:TPU:0, one launch (start us, length us, event | category | flops | bytes accessed | tf_op | source)
XLA Modules:
  0.0 136.7 jit_solution(890474260798640681)
XLA Ops:
  0.7 133.8 %shard_map.100 = f32[192,1280]{1,0:T(8,128)} custom-call(bf16[256,2048]{1,0:T(8,128)(2,1)} %gq.1, s32[1,128]{1,0:T(1,128)} %pos.1, s32[1]{0:T(128)S(6)} %copy.12.count, s32[1,128]{1,0:T(1,128)} %dest.1, f32[1,2048]{1,0:T(1,128)} %bitcast.1, bf16[1024,2048]{1,0:T(8,128)(2,1)} %wq_hbm.1, bf16[256,2048]{1,0:T(8,128)(2,1)} %em_hbm.1, bf16[256,2048]{1,0:T(8,128)(2,1)} %gr_hbm.1, ...), custom_call_target="tpu_custom_call" | custom-call | flops 13958643712 | bytes 16777216 | tf_op jit(solution)/shard_map/pallas_call | solution.py:623
  134.5 2.2 %copy.13 = f32[192,1280]{1,0:T(8,128)} copy(f32[192,1280]{1,0:T(8,128)} %shard_map.100) | data formatting | bytes 1966080

commit v7 on v5

--- a/solution.py
+++ b/solution.py
@@ -192,13 +192,17 @@
         b = zz * CORES + c
         right, left, side = kinds
 
-        @pl.when((zz <= z) & (z < Z - 1))
+        @pl.when((zz <= z) & (z < Z - 1) & (c == 0))
         def _():
             act(right(b, d))
 
         @pl.when((zz >= z) & (z > 0))
         def _():
             act(left(b, d))
+
+        @pl.when((zz <= z) & (z < Z - 1) & (c == 1))
+        def _():
+            act(right(b, d))
 
         act(side(b, d))
 
@@ -209,7 +213,7 @@
         copy.wait_send()
 
     def peer(k):
-        return (t + k) % PARTS
+        return (t + k + c * (PARTS - 2 * k)) % PARTS
 
     def arrived(ref, sem):
         remote(ref, ref, x_s.at[0, 0, 0], sem, sibling).wait_recv()
@@ -475,6 +479,45 @@
                     u_copy(zz, e, (s + k) % groups).start()
                 w[pl.ds(s, 1), pl.ds(zz, 1), e] = u[zz, e, s][None, None]
 
+    def f_copy(b, zz, e):
+        j = tile_of(zz, e)
+        return remote(
+            w.at[b, zz, e], f.at[zz, b % 2, j], w_s.at[b, zz, e], f_r.at[zz, b % 2, j], (s, b // 2)
+        )
+
+    def hand_out(i, carry):
+        step, k = i // groups, i % groups
+        b = (s + k) % groups
+        zz = stage_order(b // CORES, step)
+        for e in range(2):
+            @pl.when(held(zz, e))
+            def _():
+                @pl.when(b != s)
+                def _():
+                    arrived(w.at[b, zz, e], w_r.at[b, zz, e])
+
+                @pl.when(b // 2 != t)
+                def _():
+                    f_copy(b, zz, e).start()
+
+                @pl.when(b // 2 == t)
+                def _():
+                    f[pl.ds(zz, 1), pl.ds(b % 2, 1), pl.ds(tile_of(zz, e), 1)] = w[b, zz, e][None, None, None]
+
+        return carry
+
+    def first_sent(zz, carry):
+        for d in range(2):
+            spread(sent, x_kinds, zz, d)
+            for k in range(1, PARTS):
+                sent(part_copy(d, zz, k))
+            for cc in range(CORES):
+                @pl.when((zz != z) | (c != cc))
+                def _():
+                    sent(sums_copy(d, zz, cc))
+
+        return carry
+
     def second_step(i, carry):
         step, d = i // 2, i % 2
         zz = stage_order(z, step)
@@ -509,39 +552,24 @@
         def _():
             add_tiles(stage_order(z, step - 1))
 
+        @pl.when(i == 6)
+        def _():
+            lax.fori_loop(0, 2 * groups, hand_out, 0)
+            lax.fori_loop(0, Z, first_sent, 0)
+            for k in range(1, groups):
+                sent(at_copy(k))
+            for d in range(2):
+                for k in range(1, PARTS):
+                    sent(grad_copy(d, k))
+                    sent(stat_copy(d, k))
+
+
         return carry
 
     lax.fori_loop(0, 2 * Z, second_step, 0)
     add_tiles(stage_order(z, Z - 1))
 
-    def f_copy(b, zz, e):
-        j = tile_of(zz, e)
-        return remote(
-            w.at[b, zz, e], f.at[zz, b % 2, j], w_s.at[b, zz, e], f_r.at[zz, b % 2, j], (s, b // 2)
-        )
-
-    def hand_out(i, carry):
-        step, k = i // groups, i % groups
-        b = (s + k) % groups
-        zz = stage_order(b // CORES, step)
-        for e in range(2):
-            @pl.when(held(zz, e))
-            def _():
-                @pl.when(b != s)
-                def _():
-                    arrived(w.at[b, zz, e], w_r.at[b, zz, e])
-
-                @pl.when(b // 2 != t)
-                def _():
-                    f_copy(b, zz, e).start()
-
-                @pl.when(b // 2 == t)
-                def _():
-                    f[pl.ds(zz, 1), pl.ds(b % 2, 1), pl.ds(tile_of(zz, e), 1)] = w[b, zz, e][None, None, None]
-
-        return carry
-
-    lax.fori_loop(0, Z * groups, hand_out, 0)
+    lax.fori_loop(2 * groups, Z * groups, hand_out, 0)
 
     def finish(zz, carry):
         span = pl.ds(pl.multiple_of(zz * pair_rows, pair_rows), pair_rows)
@@ -557,23 +585,9 @@
 
     lax.fori_loop(0, Z, finish, 0)
 
-    for k in range(1, groups):
-        sent(at_copy(k))
-    for d in range(2):
-        for k in range(1, PARTS):
-            sent(grad_copy(d, k))
-            sent(stat_copy(d, k))
-
     def all_sent(zz, carry):
         for d in range(2):
-            spread(sent, x_kinds, zz, d)
             spread(sent, h_kinds, zz, d)
-            for k in range(1, PARTS):
-                sent(part_copy(d, zz, k))
-            for cc in range(CORES):
-                @pl.when((zz != z) | (c != cc))
-                def _():
-                    sent(sums_copy(d, zz, cc))
 
         for j in range(tiles):
             @pl.when((j + zz) % PARTS != t)

time: 134 us -> 131 us (0.978)
  Pallas kernels: 131 us -> 128 us
    pallas_call x1, Pallas kernels: 131 us -> 128 us  [fused(): pl.pallas_call(functools.partial(fused_kernel, capacity), out_shape=jax.S...]
where the time goes in v7:
time: 131 us
  Pallas kernels  128 us (98%)
  local copies, waits for them, and re-layouts  2.21 us (2%)
    pallas_call x1, Pallas kernels, fused(): pl.pallas_call(functools.partial(fused_kernel, capacity), out_shape=jax.S...  128 us

profile of v7, /device:TPU:0, one launch (start us, length us, event | category | flops | bytes accessed | tf_op | source)
XLA Modules:
  0.0 131.1 jit_solution(12108197824426499477)
XLA Ops:
  0.7 128.2 %shard_map.100 = f32[192,1280]{1,0:T(8,128)} custom-call(bf16[256,2048]{1,0:T(8,128)(2,1)} %gq.1, s32[1,128]{1,0:T(1,128)} %pos.1, s32[1]{0:T(128)S(6)} %copy.12.count, s32[1,128]{1,0:T(1,128)} %dest.1, f32[1,2048]{1,0:T(1,128)} %bitcast.1, bf16[1024,2048]{1,0:T(8,128)(2,1)} %wq_hbm.1, bf16[256,2048]{1,0:T(8,128)(2,1)} %em_hbm.1, bf16[256,2048]{1,0:T(8,128)(2,1)} %gr_hbm.1, ...), custom_call_target="tpu_custom_call" | custom-call | flops 13958643712 | bytes 16777216 | tf_op jit(solution)/shard_map/pallas_call | solution.py:646
  128.9 2.2 %copy.13 = f32[192,1280]{1,0:T(8,128)} copy(f32[192,1280]{1,0:T(8,128)} %shard_map.100) | data formatting | bytes 1966080

commit v8 on v7

--- a/solution.py
+++ b/solution.py
@@ -124,9 +124,9 @@
 
 def fused_kernel(
     capacity,
-    gq, pos, count, dest, gain, wq_hbm, em_hbm, gr_hbm, wm_hbm, mp_hbm,
+    gq, pos, count, dest, gain, wq_hbm, em_hbm, gr_hbm, wm_hbm,
     out,
-    wq, em, gr, wm, mp, slope, wq_t, wm_t,
+    wq, em, gr, wm,
     x, part, part_in, sums, grads,
     em_rows, gr_rows, ng, stat, rows_at,
     h, q, q_in, u, w, f,
@@ -155,7 +155,7 @@
     loads = [
         pltpu.make_async_copy(src, dst, local_sem.at[i])
         for i, (src, dst) in enumerate(
-            ((wq_hbm, wq), (em_hbm, em), (gr_hbm, gr), (wm_hbm, wm), (mp_hbm, mp))
+            ((wq_hbm, wq), (em_hbm, em), (gr_hbm, gr), (wm_hbm, wm))
         )
     ]
     for load in loads:
@@ -332,12 +332,7 @@
                 h[pl.ds(s, 1), d, p * rows:(p + 1) * rows, lo:lo + block] = result.astype(BF16)[None]
         spread(start, h_kinds, z, d)
 
-    def turn(src, dst):
-        for lo in range(0, src.shape[0], TILE):
-            dst[:, lo:lo + TILE] = src[lo:lo + TILE].T
-
     loads[0].wait()
-    turn(wq, wq_t)
     pass_on(x, x_r, x_kinds, stage_order(z, 1), 0)
 
     @pl.when(middle)
@@ -373,7 +368,7 @@
         left = x[pl.ds(zz * CORES, CORES), pl.ds(d, 1)].reshape(CORES * half, -1)
         tile = 256
         for n in range(0, block, tile):
-            piece = jnp.dot(left, wq_t[:, n:n + tile], preferred_element_type=F32).astype(BF16)
+            piece = transposed_product(left, wq[n:n + tile]).astype(BF16)
             piece = piece.reshape(CORES, PARTS, rows, tile)
             for p in range(PARTS):
                 part[pl.ds(d, 1), pl.ds(zz, 1), p, :, :, n:n + tile] = piece[:, p][None, None]
@@ -387,22 +382,6 @@
             loads[2].wait()
             gr_rows[...] = pick(gr)
 
-        @pl.when(g == 2)
-        def _():
-            loads[3].wait()
-            turn(wm, wm_t)
-
-        @pl.when(g == 4)
-        def _():
-            loads[4].wait()
-
-            def some_rows(i, carry):
-                span = pl.ds(pl.multiple_of(i * UNIT, UNIT), UNIT)
-                slope[span] = gelu_slope(mp[span])
-                return carry
-
-            lax.fori_loop(0, mp.shape[0] // UNIT, some_rows, 0)
-
         @pl.when(g == 2 * Z - 1)
         def _():
             norm_finish(0)
@@ -433,6 +412,7 @@
     for k in range(1, groups):
         b = (s + k) % groups
         arrived(rows_at.at[b], at_r.at[b])
+    loads[3].wait()
 
     def first_tile(zz):
         return (t + PARTS - zz) % PARTS
@@ -536,7 +516,7 @@
         left = h[pl.ds(zz * CORES, CORES), pl.ds(d, 1)].reshape(CORES * half, -1)
         for j in range(0, tiles, 2):
             hi = min(j + 2, tiles)
-            piece = jnp.dot(left, wm_t[:, j * TILE:hi * TILE], preferred_element_type=F32).astype(BF16)
+            piece = transposed_product(left, wm[j * TILE:hi * TILE]).astype(BF16)
             for jj in range(j, hi):
                 q[pl.ds(zz, 1), pl.ds(d, 1), jj] = piece[:, (jj - j) * TILE:(jj - j + 1) * TILE][None, None]
         for j in range(tiles):
@@ -580,7 +560,7 @@
                     arrived(f.at[zz, side, j], f_r.at[zz, side, j])
 
                 lo = side * hidden + j * TILE
-                out[span, lo:lo + TILE] = f[zz, side, j].astype(F32) * slope[span, lo:lo + TILE]
+                out[span, lo:lo + TILE] = f[zz, side, j]
         return carry
 
     lax.fori_loop(0, Z, finish, 0)
@@ -625,8 +605,7 @@
     anywhere = pl.BlockSpec(memory_space=pl.ANY)
     scratch = [
         vmem(query_weight.shape, BF16), vmem(embeds.shape, BF16), vmem(grad_resid.shape, BF16),
-        vmem(merge_weight.shape, BF16), vmem(merge_pre.shape, BF16), vmem(merge_pre.shape, F32),
-        vmem(query_weight.shape[::-1], BF16), vmem(merge_weight.shape[::-1], BF16),
+        vmem(merge_weight.shape, BF16),
         vmem((groups, 2, half, columns), BF16),
         vmem((2, Z, PARTS, CORES, rows, block), BF16), vmem((2, Z, PARTS, CORES, rows, block), BF16),
         vmem((2, Z, CORES, rows, block), BF16), vmem((2, groups, rows, block), BF16),
@@ -643,12 +622,12 @@
         dma((groups, 2, 3)), dma((groups, 2)), dma((Z, 2, tiles)), dma((Z, 2, 2, PARTS)),
         dma((Z, 2, groups)), dma((groups, Z, 2)), dma((groups, Z, 2)), dma((Z, 2, tiles)),
     ]
-    return pl.pallas_call(
+    hidden_grad = pl.pallas_call(
         functools.partial(fused_kernel, capacity),
-        out_shape=jax.ShapeDtypeStruct(merge_pre.shape, F32),
+        out_shape=jax.ShapeDtypeStruct(merge_pre.shape, BF16),
         in_specs=[
             in_vmem, in_vmem, pl.BlockSpec(memory_space=pltpu.SMEM), in_vmem, in_vmem,
-            anywhere, anywhere, anywhere, anywhere, anywhere,
+            anywhere, anywhere, anywhere, anywhere,
         ],
         out_specs=in_vmem,
         scratch_shapes=scratch,
@@ -658,12 +637,13 @@
         cost_estimate=pl.CostEstimate(
             flops=4 * groups * image_count * columns * (block + merge_weight.shape[0]),
             bytes_accessed=16 * 1024 * 1024,
-            transcendentals=merge_pre.size,
+            transcendentals=0,
         ),
     )(
         grad_query, img_pos, img_count, img_dest, norm_gain.reshape(1, -1),
-        query_weight, embeds, grad_resid, merge_weight, merge_pre,
+        query_weight, embeds, grad_resid, merge_weight,
     )
+    return hidden_grad.astype(F32) * gelu_slope(merge_pre)
 
 
 def solution(mesh):

time: 131 us -> 135 us (1.031)
  Pallas kernels: 128 us -> 131 us
  other arithmetic: 0 us -> 2.42 us
  local copies, waits for them, and re-layouts: 2.21 us -> 0.01 us
    pallas_call x1, Pallas kernels: 128 us -> 131 us  [fused(): pl.pallas_call(functools.partial(fused_kernel, capacity), out_shape=jax.S...]
    mul x0 -> x1, other arithmetic: none -> 2.42 us  [fused(): return hidden_grad.astype(F32) * gelu_slope(merge_pre)]
    unnamed x1 -> x2, local copies, waits for them, and re-layouts: 2.21 us -> 0.01 us
where the time goes in v8:
time: 135 us; the launch traced here: 134 us
  Pallas kernels  131 us (97%)
  other arithmetic  2.42 us (2%)
    pallas_call x1, Pallas kernels, fused(): pl.pallas_call(functools.partial(fused_kernel, capacity), out_shape=jax.S...  131 us

profile of v8, /device:TPU:0, one launch (start us, length us, event | category | flops | bytes accessed | tf_op | source)
XLA Modules:
  0.0 134.3 jit_solution(1903476023473535693)
XLA Ops:
  0.7 0.0 copy-start
  0.7 131.2 %shard_map.100 = bf16[192,1280]{1,0:T(8,128)(2,1)} custom-call(bf16[256,2048]{1,0:T(8,128)(2,1)} %gq.1, s32[1,128]{1,0:T(1,128)} %pos.1, s32[1]{0:T(128)S(6)} %copy.11.count, s32[1,128]{1,0:T(1,128)} %dest.1, f32[1,2048]{1,0:T(1,128)} %bitcast.1, bf16[1024,2048]{1,0:T(8,128)(2,1)} %wq_hbm.1, bf16[256,2048]{1,0:T(8,128)(2,1)} %em_hbm.1, ...), custom_call_target="tpu_custom_call" | custom-call | flops 13958643712 | bytes 16777216 | tf_op jit(solution)/shard_map/pallas_call | solution.py:625
  131.9 0.0 copy-done
  131.9 2.4 %fusion.4 = f32[192,1280]{1,0:T(8,128)} fusion(bf16[192,1280]{1,0:T(8,128)(2,1)S(1)} %copy-done, bf16[192,1280]{1,0:T(8,128)(2,1)} %shard_map.100), kind=kLoop, calls=%fused_computation.8 | loop fusion | flops 2703360 | bytes 1966080 | tf_op jit(solution)/shard_map/mul | solution.py:646
Async XLA Ops:
  0.7 131.3 %copy-start = (bf16[192,1280]{1,0:T(8,128)(2,1)S(1)}, bf16[192,1280]{1,0:T(8,128)(2,1)}, u32[]{:S(2)}) copy-start(bf16[192,1280]{1,0:T(8,128)(2,1)} %param.19) | copy-start | bytes 1474564
